TPU v7x, 32 devices: a whole 2x2x4 slice. The times are simulated.
32 devices in a mesh: ma: 8 (over y, x, core), row: 4 (over z).
Axes of the slice: x: 2, y: 2, z: 4, core: 2. Of those that a mesh axis runs over, the one named last changes fastest.
Arguments:
- velocity: bfloat16 [3, 2, 384, 128, 384], P(None, None, 'ma', 'row'), may hold values from -6 to 6
- vorticity: bfloat16 [3, 2, 384, 128, 384], P(None, None, 'ma', 'row'), may hold values from -6 to 6
- order_table: int32 [384], replicated, may hold values from 0 to 383, as said below
- legendre_bf: bfloat16 [384, 384, 576], P('ma'), may hold values from -24 to 24, as said below
- weighted: bfloat16 [384, 384, 576], P('ma'), may hold values from -1 to 1, as said below
- inverse_operators: float32 [384, 128, 128], P('row'), may hold values from -1.5 to 1.5
Outputs:
- advanced: float32 [3, 2, 384, 384, 128], P(None, None, 'ma', 'row')
Inputs may be any that keep to these rules, and one draw needn't show every extreme that they name: `order_table`: slots 2k and 2k + 1 hold wavenumbers that add up to 383, and every wavenumber from 0 to 383 stands in exactly one slot. legendre_bf[slot, l, j] is Pbar_l^m(x_j) rounded to bfloat16, with m = order_table[slot], x_j = cos(pi (j + 0.5) / 576), s_j = sin(pi (j + 0.5) / 576), zero for l < m, Pbar_m^m = exp(-0.5 log 2 + 0.5 (lgamma(m + 1.5) - lgamma(m + 1) - lgamma(1.5)) + m log s_j) and Pbar_l^m = a (x_j Pbar_(l-1)^m - b Pbar_(l-2)^m), a = sqrt((4 l^2 - 1) / (l^2 - m^2)), b = sqrt(((l - 1)^2 - m^2) / (4 (l - 1)^2 - 1)). weighted[slot, l, j] is w_j Pbar_l^m(x_j), computed in float32 and rounded to bfloat16, with w_j = pi s_j / 576.
All inputs are finite; a program needn't handle non-finite values.
Results may differ from a plain program's by a relative error of at most 0.005.
Values may be sent and summed in bfloat16 or wider, within the bound.
A program may use at most 256 MiB of HBM per device.

v0:
```python
import math

import jax
import jax.numpy as jnp
from jax import lax
from jax.sharding import PartitionSpec as P

NL = 384
NLAT = 576
NLON = 1152
NR = 128


time_step = 0.5
rotation = 2.0


def longitude_table(orders):
    points = jnp.arange(NLON, dtype=jnp.int32)
    phases = orders[:, None] * points[None, :] % NLON
    angles = phases.astype(jnp.float32) * (2.0 * math.pi / NLON)
    return jnp.stack([jnp.cos(angles), -jnp.sin(angles)]).astype(jnp.bfloat16)


def cross_terms(moving, spinning):
    spin_total = spinning[2] + rotation
    component_one = moving[1] * spin_total - moving[2] * spinning[1]
    component_two = moving[2] * spinning[0] - moving[0] * spin_total
    component_three = moving[0] * spinning[1] - moving[1] * spinning[0]
    return jnp.stack([component_one, component_two, component_three])


def per_device(velocity, vorticity, order_table, legendre_bf, weighted, inverse_operators):
    slot_count = velocity.shape[2]
    radius_count = velocity.shape[3]
    degree_count = inverse_operators.shape[0]
    own_orders = lax.dynamic_slice_in_dim(
        order_table, lax.axis_index("ma") * slot_count, slot_count
    )
    own_scale = jnp.where(own_orders == 0, 1.0, 2.0).astype(jnp.float32) / NL
    harmonics = longitude_table(order_table)

    def arrange(grid_values):
        scaled = (grid_values * own_scale[None, None, :, None, None]).astype(jnp.bfloat16)
        ordered = jnp.transpose(scaled, (0, 1, 2, 4, 3))
        return ordered.reshape(3, 2, slot_count, NLAT * radius_count)

    def synthesize(spectral):
        grid_values = jnp.einsum(
            "cpsrl,slt->cpsrt", spectral, legendre_bf, preferred_element_type=jnp.float32
        )
        return arrange(grid_values)

    def to_longitude(pieces):
        return jnp.einsum("cpsk,psn->ckn", pieces, harmonics, preferred_element_type=jnp.float32)

    velocity_grid = to_longitude(
        lax.all_to_all(synthesize(velocity), "ma", split_axis=3, concat_axis=2, tiled=True)
    )
    vorticity_grid = to_longitude(
        lax.all_to_all(synthesize(vorticity), "ma", split_axis=3, concat_axis=2, tiled=True)
    )
    products = cross_terms(velocity_grid, vorticity_grid).astype(jnp.bfloat16)
    spectral_back = jnp.einsum(
        "ckn,psn->cpsk", products, harmonics, preferred_element_type=jnp.float32
    )
    spectral_back = (NL / NLON * spectral_back).astype(jnp.bfloat16)
    pieces = lax.all_to_all(spectral_back, "ma", split_axis=2, concat_axis=3, tiled=True)
    field_count = pieces.shape[0]
    split_pieces = pieces.reshape(field_count, 2, slot_count, NLAT, radius_count)
    terms = jnp.einsum(
        "cpstr,slt->cpslr", split_pieces, weighted, preferred_element_type=jnp.float32
    )
    spec_terms = terms.reshape(field_count, 2, slot_count, NL * radius_count)
    velocity_terms = jnp.transpose(velocity.astype(jnp.float32), (0, 1, 2, 4, 3)).reshape(
        3, 2, slot_count, NL * radius_count
    )
    right_side = velocity_terms + time_step * spec_terms
    right_side = right_side.reshape(3, 2, slot_count, 1, NL * radius_count)
    operator_blocks = inverse_operators.reshape(degree_count, NR, NR // radius_count, radius_count)
    pieces = lax.all_to_all(
        right_side.astype(jnp.bfloat16), "row", split_axis=4, concat_axis=3, tiled=True
    ).astype(right_side.dtype)
    field_count = pieces.shape[0]
    columns = pieces.reshape(
        field_count, 2, slot_count, NR // radius_count, degree_count, radius_count
    )
    return jnp.einsum(
        "cpsqlr,laqr->cpsla", columns, operator_blocks, precision=lax.Precision.HIGHEST
    )


def solution(mesh):
    in_specs = (
        P(None, None, "ma", "row", None),
        P(None, None, "ma", "row", None),
        P(),
        P("ma", None, None),
        P("ma", None, None),
        P("row", None, None),
    )
    out_specs = P(None, None, "ma", "row", None)
    return jax.shard_map(
        per_device, mesh=mesh, in_specs=in_specs, out_specs=out_specs, check_vma=False
    )
```

profile of v0, /device:TPU:0, one launch (start us, length us, event | category | flops | bytes accessed | tf_op | source)
XLA Modules:
  0.0 1133.7 jit_solution(13620141383285390422)
XLA Ops:
  0.8 18.7 %fusion.16 = bf16[3,2,48,576,32]{3,4,1,0,2:T(8,128)(2,1)} fusion(f32[48]{0:T(128)S(1)} %fusion.41, bf16[3,2,48,32,384]{4,3,2,1,0:T(8,128)(2,1)} %param.7, bf16[48,384,576]{1,2,0:T(8,128)(2,1)} %param.9), kind=kOutput, calls=%fused_computation.23 | convolution fusion | flops 4087480320 | bytes 38928576 | tf_op jit(solution)/shard_map/cpsrl,slt->cpsrt/dot_general | solution.py:49
  19.5 51.0 %copy.84 = bf16[3,2,48,576,32]{2,1,0,4,3:T(2,128)(2,1)} copy(bf16[3,2,48,576,32]{3,4,1,0,2:T(8,128)(2,1)} %fusion.16) | data formatting | bytes 21233664 | tf_op jit(solution)/shard_map/reshape | solution.py:46
  70.5 44.9 %reshape.150 = bf16[8,2,331776]{2,1,0:T(2,128)(2,1)} reshape(bf16[18432,3,2,48]{3,2,1,0:T(2,128)(2,1)} %bitcast.89) | data formatting | bytes 21233664
  120.8 18.8 %fusion.15 = bf16[3,2,48,576,32]{3,4,1,0,2:T(8,128)(2,1)} fusion(f32[48]{0:T(128)S(1)} %fusion.41, bf16[48,384,576]{1,2,0:T(8,128)(2,1)} %param.9, bf16[3,2,48,32,384]{4,3,2,1,0:T(8,128)(2,1)} %param.6), kind=kOutput, calls=%fused_computation.22 | convolution fusion | flops 4087480320 | bytes 38928576 | tf_op jit(solution)/shard_map/cpsrl,slt->cpsrt/dot_general | solution.py:49
  139.6 51.0 %copy.81 = bf16[3,2,48,576,32]{2,1,0,4,3:T(2,128)(2,1)} copy(bf16[3,2,48,576,32]{3,4,1,0,2:T(8,128)(2,1)} %fusion.15) | data formatting | bytes 21233664 | tf_op jit(solution)/shard_map/reshape | solution.py:46
  190.6 45.0 %reshape.148 = bf16[8,2,331776]{2,1,0:T(2,128)(2,1)} reshape(bf16[18432,3,2,48]{3,2,1,0:T(2,128)(2,1)} %bitcast.90) | data formatting | bytes 21233664
  252.9 29.2 %reshape.151 = bf16[18432,3,2,48]{3,2,1,0:T(2,128)(2,1)} reshape(bf16[8,2,331776]{2,1,0:T(2,128)(2,1)} %all-to-all-done.1) | data formatting | bytes 21233664
  282.1 60.1 %copy.86 = bf16[3,2,48,8,2304]{4,2,3,1,0:T(8,128)(2,1)} copy(bf16[3,2,48,8,2304]{2,1,0,4,3:T(2,128)(2,1)} %bitcast.91) | data formatting | bytes 21233664 | tf_op jit(solution)/shard_map/all_to_all | solution.py:61
  342.2 20.6 %all-to-all-done = bf16[8,2,331776]{2,1,0:T(2,128)(2,1)} async-done(((bf16[8,2,331776]{2,1,0:T(2,128)(2,1)}), bf16[8,2,331776]{2,1,0:T(2,128)(2,1)}, u32[]{:S(2)}, u32[]{:S(2)}) %all-to-all-start) | async-done | bytes 10616864 | tf_op jit(solution)/shard_map/all_to_all | solution.py:58
  362.8 29.2 %reshape.149 = bf16[18432,3,2,48]{3,2,1,0:T(2,128)(2,1)} reshape(bf16[8,2,331776]{2,1,0:T(2,128)(2,1)} %all-to-all-done) | data formatting | bytes 21233664
  392.0 60.2 %copy.83 = bf16[3,2,48,8,2304]{4,2,3,1,0:T(8,128)(2,1)} copy(bf16[3,2,48,8,2304]{2,1,0,4,3:T(2,128)(2,1)} %bitcast.92) | data formatting | bytes 21233664 | tf_op jit(solution)/shard_map/all_to_all | solution.py:58
  452.2 21.0 %convolution_bitcast_fusion = f32[3,2304,1152]{2,1,0:T(8,128)} fusion(bf16[3,2,384,2304]{3,2,1,0:T(8,128)(2,1)} %bitcast.97, bf16[1,384,1152]{2,1,0:T(8,128)(2,1)S(1)} %get-tuple-element.9, bf16[1,384,1152]{2,1,0:T(8,128)(2,1)S(1)} %get-tuple-element.8), kind=kOutput, calls=%fused_computation.2 | convolution fusion | flops 12231475200 | bytes 44236800 | tf_op jit(solution)/shard_map/cpsk,psn->ckn/dot_general | solution.py:55
  473.2 21.3 %convolution_bitcast_fusion.1 = f32[3,2304,1152]{2,1,0:T(8,128)} fusion(bf16[3,2,384,2304]{3,2,1,0:T(8,128)(2,1)} %bitcast.98, bf16[1,384,1152]{2,1,0:T(8,128)(2,1)S(1)} %get-tuple-element.9, bf16[1,384,1152]{2,1,0:T(8,128)(2,1)S(1)} %get-tuple-element.8), kind=kOutput, calls=%fused_computation.3 | convolution fusion | flops 12231475200 | bytes 44236800 | tf_op jit(solution)/shard_map/cpsk,psn->ckn/dot_general | solution.py:55
  494.5 27.3 %subtract_convert_fusion.2 = (bf16[1,2304,1152]{2,1,0:T(8,128)(2,1)}, bf16[1,2304,1152]{2,1,0:T(8,128)(2,1)}, bf16[1,2304,1152]{2,1,0:T(8,128)(2,1)}) fusion(f32[3,2304,1152]{2,1,0:T(8,128)} %convolution_bitcast_fusion, f32[3,2304,1152]{2,1,0:T(8,128)} %convolution_bitcast_fusion.1), kind=kLoop, calls=%fused_computation.29 | loop fusion | flops 34504704 | bytes 79626240 | tf_op jit(solution)/shard_map/convert.1
  538.7 79.6 %copy.62 = bf16[3,2,384,2304]{3,1,0,2:T(2,128)(2,1)S(1)} copy(bf16[3,2,384,2304]{3,2,0,1:T(8,128)(2,1)S(1)} %fusion.17) | data formatting | bytes 21233664 | tf_op jit(solution)/shard_map/convert_element_type | solution.py:67
  618.3 120.7 %all_to_all.60 = bf16[3,2,384,2304]{3,1,0,2:T(2,128)(2,1)S(1)} all-to-all(bf16[3,2,384,2304]{3,1,0,2:T(2,128)(2,1)S(1)} %copy.62), channel_id=1, replica_groups=mesh['ma'=8,'row'=4] {'ma'}, dimensions={2} | all-to-all | bytes 21233664 | tf_op jit(solution)/shard_map/all_to_all | solution.py:68
  746.5 46.3 %reshape.137 = bf16[3,2,48,576,32]{4,3,2,1,0:T(8,128)(2,1)} reshape(bf16[3,2,48,8,2304]{4,3,2,1,0:T(8,128)(2,1)} %bitcast.94) | data formatting | bytes 21233664 | tf_op jit(solution)/shard_map/reshape | solution.py:70
  792.8 27.9 %fusion.14 = bf16[3,2,48,384,32]{3,4,1,0,2:T(8,128)(2,1)} fusion(bf16[48,384,576]{1,2,0:T(8,128)(2,1)} %param.10, bf16[3,2,48,576,32]{4,3,2,1,0:T(8,128)(2,1)} %reshape.137, bf16[3,2,48,32,384]{4,3,2,1,0:T(8,128)(2,1)} %param.6), kind=kOutput, calls=%fused_computation.21 | convolution fusion | flops 4091019264 | bytes 46006272 | tf_op jit(solution)/shard_map/cpstr,slt->cpslr/dot_general | solution.py:71
  820.7 31.5 %copy.88 = bf16[3,2,48,384,32]{2,1,0,4,3:T(2,128)(2,1)} copy(bf16[3,2,48,384,32]{3,4,1,0,2:T(8,128)(2,1)} %fusion.14) | data formatting | bytes 14155776 | tf_op jit(solution)/shard_map/convert_element_type | solution.py:82
  852.2 42.5 %reshape.152 = bf16[4,2,442368]{2,1,0:T(2,128)(2,1)} reshape(bf16[12288,1,3,2,48]{4,3,2,1,0:T(2,128)(2,1)} %bitcast.93) | data formatting | bytes 14155776
  907.2 149.0 %all-to-all-done.3 = bf16[4,2,442368]{2,1,0:T(2,128)(2,1)} async-done(((bf16[4,2,442368]{2,1,0:T(2,128)(2,1)}), bf16[4,2,442368]{2,1,0:T(2,128)(2,1)}, u32[]{:S(2)}, u32[]{:S(2)}) %all-to-all-start.3) | async-done | bytes 7077920 | tf_op jit(solution)/shard_map/all_to_all | solution.py:81
  1056.2 31.9 %reshape.153 = bf16[12288,1,3,2,48]{4,3,2,1,0:T(2,128)(2,1)} reshape(bf16[4,2,442368]{2,1,0:T(2,128)(2,1)} %all-to-all-done.3) | data formatting | bytes 14155776
  1088.2 26.5 %fusion.22 = f32[3,2,48,96,128]{4,2,1,0,3:T(8,128)} fusion(f32[96,128,4,32,1,1]{1,3,2,5,4,0:T(8,128)} %bitcast.99, bf16[3,2,48,4,96,32]{2,1,0,5,4,3:T(2,128)(2,1)} %bitcast.96), kind=kOutput, calls=%fused_computation.30 | convolution fusion | flops 5435817984 | bytes 27525120 | tf_op jit(solution)/shard_map/cpsqlr,laqr->cpsla/dot_general | solution.py:88
  1114.7 18.5 %copy.70 = f32[3,2,48,96,128]{4,3,2,1,0:T(8,128)} copy(f32[3,2,48,96,128]{4,2,1,0,3:T(8,128)} %fusion.22) | data formatting | bytes 28311552 | tf_op jit(solution)/shard_map/cpsqlr,laqr->cpsla/transpose | solution.py:88
  (11 shorter events, 60.3 us)
Async XLA Ops:
  115.4 123.9 %all-to-all-start.1 = ((bf16[8,2,331776]{2,1,0:T(2,128)(2,1)}), bf16[8,2,331776]{2,1,0:T(2,128)(2,1)}, u32[]{:S(2)}, u32[]{:S(2)}) async-start(bf16[8,2,331776]{2,1,0:T(2,128)(2,1)} %reshape.150), calls=%async_computation.1 | async-start | bytes 21233664 | tf_op jit(solution)/shard_map/all_to_all | solution.py:61
  235.6 9.2 copy-start
  239.4 123.4 %all-to-all-start = ((bf16[8,2,331776]{2,1,0:T(2,128)(2,1)}), bf16[8,2,331776]{2,1,0:T(2,128)(2,1)}, u32[]{:S(2)}, u32[]{:S(2)}) async-start(bf16[8,2,331776]{2,1,0:T(2,128)(2,1)} %reshape.148), calls=%async_computation | async-start | bytes 21233664 | tf_op jit(solution)/shard_map/all_to_all | solution.py:58
  894.7 161.5 %all-to-all-start.3 = ((bf16[4,2,442368]{2,1,0:T(2,128)(2,1)}), bf16[4,2,442368]{2,1,0:T(2,128)(2,1)}, u32[]{:S(2)}, u32[]{:S(2)}) async-start(bf16[4,2,442368]{2,1,0:T(2,128)(2,1)} %reshape.152), calls=%async_computation.3 | async-start | bytes 14155776 | tf_op jit(solution)/shard_map/all_to_all | solution.py:81
where the time goes:
time: 1150 us; the launch traced here: 1130 us
  local copies, waits for them, and re-layouts  635 us (55%)
  waiting for transfers between devices  173 us (15%)
  matrix products  151 us (13%)
  blocking collectives  121 us (11%)
  other arithmetic  36.1 us (3%)
  starting transfers between devices  16.7 us (1%)
    unnamed x9, local copies, waits for them, and re-layouts  229 us
    all_to_all x1, waiting for transfers between devices, per_device(): lax.all_to_all(right_side.astype(jnp.bfloat16), 'row', split_axis=4, conc...  149 us
    all_to_all x1, blocking collectives, per_device(): lax.all_to_all(spectral_back, 'ma', split_axis=2, concat_axis=3, tiled=True)  121 us
    reshape x2, local copies, waits for them, and re-layouts, arrange(): return ordered.reshape(3, 2, slot_count, NLAT * radius_count)  102 us
    convert_element_type x1, local copies, waits for them, and re-layouts, per_device(): spectral_back = (NL / NLON * spectral_back).astype(jnp.bfloat16)  79.6 us
    all_to_all x1, local copies, waits for them, and re-layouts, per_device(): lax.all_to_all(synthesize(velocity), 'ma', split_axis=3, concat_axis=2, t...  60.2 us
    all_to_all x1, local copies, waits for them, and re-layouts, per_device(): lax.all_to_all(synthesize(vorticity), 'ma', split_axis=3, concat_axis=2,...  60.1 us
    reshape x1, local copies, waits for them, and re-layouts, per_device(): pieces.reshape(field_count, 2, slot_count, NLAT, radius_count)  46.3 us
  transfers between devices with their start and end apart: 3, of which 3 were waited for; matrix products, arithmetic and copies ran while one was open for 19% of the time, Pallas kernels for 0%

commit v1 on v0

--- a/solution.py
+++ b/solution.py
@@ -1,14 +1,21 @@
+import functools
 import math
 
 import jax
 import jax.numpy as jnp
 from jax import lax
+from jax.experimental import pallas as pl
+from jax.experimental.pallas import tpu as pltpu
 from jax.sharding import PartitionSpec as P
 
 NL = 384
 NLAT = 576
 NLON = 1152
 NR = 128
+
+
+LANES = 128
+ROWS = 16
 
 
 time_step = 0.5
@@ -27,10 +34,232 @@
     component_one = moving[1] * spin_total - moving[2] * spinning[1]
     component_two = moving[2] * spinning[0] - moving[0] * spin_total
     component_three = moving[0] * spinning[1] - moving[1] * spinning[0]
-    return jnp.stack([component_one, component_two, component_three])
+    return component_one, component_two, component_three
+
+
+def synth_kernel(scale_ref, spec_ref, table_ref, early_ref, late_ref, turned):
+    comps, parts, slots, radii, degrees = spec_ref.shape
+    lat = table_ref.shape[2]
+    half = radii // 2
+    rows = comps * parts * half
+    first_slot = pl.program_id(0) * slots
+    for s in range(slots):
+        spec = spec_ref[:, :, s].reshape(2 * rows, degrees)
+        sums = jnp.dot(spec, table_ref[s], preferred_element_type=jnp.float32)
+        sums = (sums * scale_ref[first_slot + s]).reshape(comps * parts, 2, half, lat)
+        wide = jnp.concatenate(
+            [sums[:, 0].reshape(rows, lat), sums[:, 1].reshape(rows, lat)], axis=1
+        )
+        for t in range(2 * lat // LANES):
+            turned[t, pl.ds(s, rows, stride=slots), :] = wide[:, t * LANES : (t + 1) * LANES]
+    owners = half // 2
+    for i in range(comps * parts):
+        c, p = i // parts, i % parts
+        for h, out_ref in enumerate((early_ref, late_ref)):
+            for d in range(owners):
+                row = (i * half + h * owners + d) * slots
+                for t in range(2 * lat // LANES):
+                    out_ref[d, c, p, :, t * LANES : (t + 1) * LANES] = turned[
+                        t, pl.ds(row, slots), :
+                    ].astype(jnp.bfloat16)
+
+
+def synthesize(spec, table, scale):
+    comps, parts, slots, radii, degrees = spec.shape
+    lat = table.shape[2]
+    owners = radii // 4
+    shape = jax.ShapeDtypeStruct((owners, comps, parts, slots, 2 * lat), jnp.bfloat16)
+    out_spec = pl.BlockSpec((owners, comps, parts, ROWS, 2 * lat), lambda i: (0, 0, 0, i, 0))
+    rows = comps * parts * radii // 2 * ROWS
+    return pl.pallas_call(
+        synth_kernel,
+        grid=(slots // ROWS,),
+        in_specs=[
+            pl.BlockSpec(memory_space=pltpu.SMEM),
+            pl.BlockSpec((comps, parts, ROWS, radii, degrees), lambda i: (0, 0, i, 0, 0)),
+            pl.BlockSpec((ROWS, degrees, lat), lambda i: (i, 0, 0)),
+        ],
+        out_specs=[out_spec, out_spec],
+        out_shape=[shape, shape],
+        scratch_shapes=[pltpu.VMEM((2 * lat // LANES, rows, LANES), jnp.float32)],
+        compiler_params=pltpu.CompilerParams(vmem_limit_bytes=56 << 20),
+        cost_estimate=pl.CostEstimate(
+            flops=2 * spec.size * lat,
+            bytes_accessed=2 * (spec.size + table.size + spec.size * lat // degrees),
+            transcendentals=0,
+        ),
+    )(scale, spec, table)
+
+
+def grid_kernel(scale, move_ref, spin_ref, across_ref, along_ref, out_ref, packed, total):
+    owners, comps, parts, slots, wide = move_ref.shape
+    waves = owners * parts * slots
+    points = along_ref.shape[1]
+    for c in range(comps):
+        packed[:, c * wide : (c + 1) * wide] = move_ref[:, c].reshape(waves, wide)
+        packed[:, (comps + c) * wide : (comps + c + 1) * wide] = spin_ref[:, c].reshape(waves, wide)
+    step = points // 3
+    for k in range(3):
+        grid = jnp.dot(
+            across_ref[k * step : (k + 1) * step, :],
+            packed[...],
+            preferred_element_type=jnp.float32,
+        )
+        fields = [grid[:, i * wide : (i + 1) * wide] for i in range(2 * comps)]
+        products = jnp.concatenate(cross_terms(fields[:3], fields[3:]), axis=1)
+        part = jnp.dot(
+            along_ref[:, k * step : (k + 1) * step],
+            products.astype(jnp.bfloat16),
+            preferred_element_type=jnp.float32,
+        )
+        total[...] = part if k == 0 else total[...] + part
+    for c in range(comps):
+        back = (scale * total[:, c * wide : (c + 1) * wide]).astype(jnp.bfloat16)
+        out_ref[:, c] = back.reshape(owners, parts, slots, wide)
+
+
+def through_grid(moving, spinning, across, along, scale):
+    owners, comps, parts, slots, columns = moving.shape
+    waves, points = along.shape
+    wide = columns // 3
+    block = pl.BlockSpec((owners, comps, parts, slots, wide), lambda i: (0, 0, 0, 0, i))
+    return pl.pallas_call(
+        functools.partial(grid_kernel, scale),
+        grid=(columns // wide,),
+        in_specs=[
+            block,
+            block,
+            pl.BlockSpec((points, waves), lambda i: (0, 0)),
+            pl.BlockSpec((waves, points), lambda i: (0, 0)),
+        ],
+        out_specs=block,
+        out_shape=jax.ShapeDtypeStruct(moving.shape, jnp.bfloat16),
+        scratch_shapes=[
+            pltpu.VMEM((waves, 2 * comps * wide), jnp.bfloat16),
+            pltpu.VMEM((waves, comps * wide), jnp.float32),
+        ],
+        compiler_params=pltpu.CompilerParams(vmem_limit_bytes=56 << 20),
+        cost_estimate=pl.CostEstimate(
+            flops=2 * 3 * comps * waves * points * columns,
+            bytes_accessed=6 * moving.size,
+            transcendentals=0,
+        ),
+    )(moving, spinning, across, along)
+
+
+def analyze_kernel(early_ref, late_ref, table_ref, velocity_ref, out_ref, turned):
+    comps, parts, slots, radii, degrees = velocity_ref.shape
+    lat = table_ref.shape[2]
+    half = radii // 2
+    rows = comps * parts * half
+    owners = half // 2
+    for i in range(comps * parts):
+        c, p = i // parts, i % parts
+        for h, in_ref in enumerate((early_ref, late_ref)):
+            for d in range(owners):
+                row = (i * half + h * owners + d) * slots
+                for t in range(2 * lat // LANES):
+                    turned[t, pl.ds(row, slots), :] = in_ref[
+                        d, c, p, :, t * LANES : (t + 1) * LANES
+                    ].astype(jnp.float32)
+    for s in range(slots):
+        wide = jnp.concatenate(
+            [
+                turned[t, pl.ds(s, rows, stride=slots), :]
+                for t in range(2 * lat // LANES)
+            ],
+            axis=1,
+        )
+        pieces = [wide[:, :lat], wide[:, lat:]]
+        pieces = [x.astype(jnp.bfloat16).reshape(comps * parts, 1, half, lat) for x in pieces]
+        left = jnp.concatenate(pieces, axis=1).reshape(2 * rows, lat)
+        terms = lax.dot_general(
+            left, table_ref[s], (((1,), (1,)), ((), ())), preferred_element_type=jnp.float32
+        )
+        terms = terms.reshape(comps, parts, radii, degrees)
+        sides = velocity_ref[:, :, s].astype(jnp.float32) + time_step * terms
+        out_ref[:, :, s] = sides.astype(jnp.bfloat16)
+
+
+def analyze(early, late, table, velocity):
+    comps, parts, slots, radii, degrees = velocity.shape
+    lat = table.shape[2]
+    owners = radii // 4
+    block = pl.BlockSpec((owners, comps, parts, ROWS, 2 * lat), lambda i: (0, 0, 0, i, 0))
+    spec_block = pl.BlockSpec((comps, parts, ROWS, radii, degrees), lambda i: (0, 0, i, 0, 0))
+    rows = comps * parts * radii // 2 * ROWS
+    return pl.pallas_call(
+        analyze_kernel,
+        grid=(slots // ROWS,),
+        in_specs=[
+            block,
+            block,
+            pl.BlockSpec((ROWS, degrees, lat), lambda i: (i, 0, 0)),
+            spec_block,
+        ],
+        out_specs=spec_block,
+        out_shape=jax.ShapeDtypeStruct(velocity.shape, jnp.bfloat16),
+        scratch_shapes=[pltpu.VMEM((2 * lat // LANES, rows, LANES), jnp.float32)],
+        compiler_params=pltpu.CompilerParams(vmem_limit_bytes=56 << 20),
+        cost_estimate=pl.CostEstimate(
+            flops=2 * velocity.size * lat,
+            bytes_accessed=2 * (3 * velocity.size + table.size),
+            transcendentals=0,
+        ),
+    )(early, late, table, velocity)
+
+
+def radial_solve(right_side, inverse_operators):
+    comps, parts, slots, radii, degrees = right_side.shape
+    own, full = inverse_operators.shape[:2]
+    groups = full // radii
+    split = right_side.reshape(comps, parts, slots, radii, groups, own)
+    split = jnp.transpose(split, (4, 5, 0, 1, 2, 3))
+    split = split.reshape(groups, own, comps * parts * slots * radii)
+    pieces = lax.all_to_all(split, "row", split_axis=0, concat_axis=0, tiled=True)
+    columns = pieces.reshape(groups, own, comps, parts, slots, radii)
+    operators = inverse_operators.astype(jnp.bfloat16).reshape(own, full, groups, radii)
+    return jnp.einsum(
+        "qlcpsr,laqr->cpsla", columns, operators, preferred_element_type=jnp.float32
+    )
+
+
+def fits(velocity, legendre_bf, owners):
+    return (
+        velocity.shape[3] == 4 * owners
+        and velocity.shape[3] % (2 * ROWS) == 0
+        and velocity.shape[2] % ROWS == 0
+        and (2 * legendre_bf.shape[2]) % (3 * LANES) == 0
+    )
+
+
+def by_radius(velocity, vorticity, order_table, legendre_bf, weighted, inverse_operators):
+    owners = lax.axis_size("ma")
+    slots = velocity.shape[2]
+    own_orders = lax.dynamic_slice_in_dim(order_table, lax.axis_index("ma") * slots, slots)
+    scale = jnp.where(own_orders == 0, 1.0, 2.0).astype(jnp.float32) / NL
+
+    def exchange(x):
+        return lax.all_to_all(x, "ma", split_axis=0, concat_axis=0, tiled=True)
+
+    move_early, move_late = synthesize(velocity, legendre_bf, scale)
+    spin_early, spin_late = synthesize(vorticity, legendre_bf, scale)
+    move_early, spin_early = exchange(move_early), exchange(spin_early)
+    move_late, spin_late = exchange(move_late), exchange(spin_late)
+    table = longitude_table(order_table).reshape(2, owners, slots, NLON)
+    along = jnp.transpose(table, (1, 0, 2, 3)).reshape(2 * owners * slots, NLON)
+    across = jnp.transpose(along)
+    early = exchange(through_grid(move_early, spin_early, across, along, NL / NLON))
+    late = exchange(through_grid(move_late, spin_late, across, along, NL / NLON))
+    right_side = analyze(early, late, weighted, velocity)
+    return radial_solve(right_side, inverse_operators)
 
 
 def per_device(velocity, vorticity, order_table, legendre_bf, weighted, inverse_operators):
+    if fits(velocity, legendre_bf, lax.axis_size("ma")):
+        return by_radius(
+            velocity, vorticity, order_table, legendre_bf, weighted, inverse_operators
+        )
     slot_count = velocity.shape[2]
     radius_count = velocity.shape[3]
     degree_count = inverse_operators.shape[0]
@@ -60,7 +289,7 @@
     vorticity_grid = to_longitude(
         lax.all_to_all(synthesize(vorticity), "ma", split_axis=3, concat_axis=2, tiled=True)
     )
-    products = cross_terms(velocity_grid, vorticity_grid).astype(jnp.bfloat16)
+    products = jnp.stack(cross_terms(velocity_grid, vorticity_grid)).astype(jnp.bfloat16)
     spectral_back = jnp.einsum(
         "ckn,psn->cpsk", products, harmonics, preferred_element_type=jnp.float32
     )

time: 1150 us -> 750 us (0.65)
  local copies, waits for them, and re-layouts: 635 us -> 169 us
  matrix products: 151 us -> 12.1 us
  Pallas kernels: 0 us -> 120 us
  waiting for transfers between devices: 173 us -> 274 us
  other arithmetic: 36.1 us -> 8.81 us
    unnamed x9, local copies, waits for them, and re-layouts: 229 us -> 65 us
    dot_general x7 -> x1, matrix products: 151 us -> 12.1 us  [radial_solve(): jnp.einsum('qlcpsr,laqr->cpsla', columns, operators, preferred_element_ty...]
    pallas_call x0 -> x5, Pallas kernels: none -> 120 us  [the longest x2 57.6 us: through_grid(): pl.pallas_call(functools.partial(grid_kernel, scale), grid=(columns // wi...]
    all_to_all x3 -> x1, local copies, waits for them, and re-layouts: 128 us -> 11.3 us  [radial_solve(): lax.all_to_all(split, 'row', split_axis=0, concat_axis=0, tiled=True)]
    convert_element_type x2 -> x0, local copies, waits for them, and re-layouts: 111 us -> none  [the longest x1 79.6 us: per_device(): spectral_back = (NL / NLON * spectral_back).astype(jnp.bfloat16)]
    all_to_all x3 -> x5, waiting for transfers between devices: 173 us -> 274 us  [the longest x1 149 us: radial_solve(): lax.all_to_all(split, 'row', split_axis=0, concat_axis=0, tiled=True)]
    reshape x3 -> x4, local copies, waits for them, and re-layouts: 148 us -> 71.6 us  [the longest x1 33 us: radial_solve(): columns = pieces.reshape(groups, own, comps, parts, slots, radii)]
    another operation x2, other arithmetic: 35.3 us -> 8.15 us
  transfers between devices with their start and end apart: 3 -> 5, of which waited for: 3 -> 5; matrix products, arithmetic and copies ran while one was open for 19% -> 6% of each run, Pallas kernels for 0% -> 11%
where the time goes in v1:
time: 750 us; the launch traced here: 740 us
  waiting for transfers between devices  274 us (37%)
  local copies, waits for them, and re-layouts  169 us (23%)
  blocking collectives  130 us (17%)
  Pallas kernels  120 us (16%)
  starting transfers between devices  25.2 us (3%)
  matrix products  12.1 us (2%)
  other arithmetic  8.81 us (1%)
    all_to_all x1, waiting for transfers between devices, radial_solve(): lax.all_to_all(split, 'row', split_axis=0, concat_axis=0, tiled=True)  149 us
    all_to_all x2, blocking collectives, exchange(): return lax.all_to_all(x, 'ma', split_axis=0, concat_axis=0, tiled=True)  130 us
    all_to_all x4, waiting for transfers between devices, exchange(): return lax.all_to_all(x, 'ma', split_axis=0, concat_axis=0, tiled=True)  125 us
    unnamed x9, local copies, waits for them, and re-layouts  65 us
    pallas_call x2, Pallas kernels, through_grid(): pl.pallas_call(functools.partial(grid_kernel, scale), grid=(columns // wi...  57.6 us
    pallas_call x2, Pallas kernels, synthesize(): pl.pallas_call(synth_kernel, grid=(slots // ROWS,), in_specs=[pl.BlockSpe...  41.1 us
    reshape x1, local copies, waits for them, and re-layouts, radial_solve(): columns = pieces.reshape(groups, own, comps, parts, slots, radii)  33 us
    reshape x2, local copies, waits for them, and re-layouts, radial_solve(): split = right_side.reshape(comps, parts, slots, radii, groups, own)  27.2 us
  transfers between devices with their start and end apart: 5, of which 5 were waited for; matrix products, arithmetic and copies ran while one was open for 6% of the time, Pallas kernels for 11%

profile of v1, /device:TPU:0, one launch (start us, length us, event | category | flops | bytes accessed | tf_op | source)
XLA Modules:
  0.0 739.9 jit_solution(9221202545602735176)
XLA Ops:
  0.0 30.4 %copy.33.table_ref = bf16[48,384,576]{2,1,0:T(8,128)(2,1)} copy(bf16[48,384,576]{1,2,0:T(8,128)(2,1)} %param.9) | data formatting | bytes 42467328 | tf_op args[3]
  31.1 20.5 %shard_map.64 = (bf16[8,3,2,48,1152]{4,3,2,1,0:T(8,128)(2,1)}, bf16[8,3,2,48,1152]{4,3,2,1,0:T(8,128)(2,1)}) custom-call(f32[48]{0:T(128)} %fusion.5.scale_ref, bf16[3,2,48,32,384]{4,3,2,1,0:T(8,128)(2,1)} %velocity_ref.1, bf16[48,384,576]{2,1,0:T(8,128)(2,1)} %copy.33.table_ref), custom_call_target="tpu_custom_call" | custom-call | flops 4076863488 | bytes 38928384 | tf_op jit(solution)/shard_map/pallas_call | solution.py:74
  51.6 5.2 all-to-all-start.3
  56.8 20.5 %shard_map.65 = (bf16[8,3,2,48,1152]{4,3,2,1,0:T(8,128)(2,1)}, bf16[8,3,2,48,1152]{4,3,2,1,0:T(8,128)(2,1)}) custom-call(f32[48]{0:T(128)} %fusion.5.scale_ref, bf16[3,2,48,32,384]{4,3,2,1,0:T(8,128)(2,1)} %spec_ref.3, bf16[48,384,576]{2,1,0:T(8,128)(2,1)} %copy.33.table_ref), custom_call_target="tpu_custom_call" | custom-call | flops 4076863488 | bytes 38928384 | tf_op jit(solution)/shard_map/pallas_call | solution.py:74
  77.3 40.7 %all-to-all-done.3.move_ref = bf16[8,3,2,48,1152]{4,3,2,1,0:T(8,128)(2,1)} async-done(((bf16[8,3,2,48,1152]{4,3,2,1,0:T(8,128)(2,1)}), bf16[8,3,2,48,1152]{4,3,2,1,0:T(8,128)(2,1)}, u32[]{:S(2)}, u32[]{:S(2)}) %all-to-all-start.3) | async-done | bytes 5308448 | tf_op jit(solution)/shard_map/all_to_all | solution.py:243
  118.0 65.9 %all_to_all.35.spin_ref = bf16[8,3,2,48,1152]{4,3,2,1,0:T(8,128)(2,1)} all-to-all(bf16[8,3,2,48,1152]{4,3,2,1,0:T(8,128)(2,1)} %get-tuple-element.12), channel_id=1, replica_groups=mesh['ma'=8,'row'=4] {'ma'}, dimensions={0} | all-to-all | bytes 10616832 | tf_op jit(solution)/shard_map/all_to_all | solution.py:243
  183.9 64.3 %all_to_all.36.move_ref = bf16[8,3,2,48,1152]{4,3,2,1,0:T(8,128)(2,1)} all-to-all(bf16[8,3,2,48,1152]{4,3,2,1,0:T(8,128)(2,1)S(1)} %copy-done.1), channel_id=1, replica_groups=mesh['ma'=8,'row'=4] {'ma'}, dimensions={0} | all-to-all | bytes 10616832 | tf_op jit(solution)/shard_map/all_to_all | solution.py:243
  253.2 8.0 %cosine_convert_fusion = (bf16[1,8,48,1152]{3,2,0,1:T(8,128)(2,1)S(1)}, bf16[1,8,48,1152]{3,2,0,1:T(8,128)(2,1)S(1)}) fusion(s32[8,48]{1,0:T(8,128)S(1)} %mul.51), kind=kLoop, calls=%fused_computation.6 | loop fusion | flops 5308416 | bytes 1771008 | tf_op jit(solution)/shard_map/convert
  263.9 28.9 %shard_map.67 = bf16[8,3,2,48,1152]{4,3,2,1,0:T(8,128)(2,1)} custom-call(bf16[8,3,2,48,1152]{4,3,2,1,0:T(8,128)(2,1)} %all-to-all-done.3.move_ref, bf16[8,3,2,48,1152]{4,3,2,1,0:T(8,128)(2,1)} %all_to_all.35.spin_ref, bf16[1152,768]{1,0:T(8,128)(2,1)} %copy.35.across_ref, bf16[768,1152]{1,0:T(8,128)(2,1)} %bitcast.27), custom_call_target="tpu_custom_call" | custom-call | flops 18345885696 | bytes 15925248 | tf_op jit(solution)/shard_map/pallas_call | solution.py:126
  292.7 21.4 %all-to-all-done.1.spin_ref = bf16[8,3,2,48,1152]{4,3,2,1,0:T(8,128)(2,1)} async-done(((bf16[8,3,2,48,1152]{4,3,2,1,0:T(8,128)(2,1)}), bf16[8,3,2,48,1152]{4,3,2,1,0:T(8,128)(2,1)}, u32[]{:S(2)}, u32[]{:S(2)}) %all-to-all-start.1) | async-done | bytes 5308448 | tf_op jit(solution)/shard_map/all_to_all | solution.py:243
  318.8 28.8 %shard_map.66 = bf16[8,3,2,48,1152]{4,3,2,1,0:T(8,128)(2,1)} custom-call(bf16[8,3,2,48,1152]{4,3,2,1,0:T(8,128)(2,1)} %all_to_all.36.move_ref, bf16[8,3,2,48,1152]{4,3,2,1,0:T(8,128)(2,1)} %all-to-all-done.1.spin_ref, bf16[1152,768]{1,0:T(8,128)(2,1)} %copy.35.across_ref, bf16[768,1152]{1,0:T(8,128)(2,1)} %bitcast.28), custom_call_target="tpu_custom_call" | custom-call | flops 18345885696 | bytes 15925248 | tf_op jit(solution)/shard_map/pallas_call | solution.py:126
  347.6 32.3 %all-to-all-done.5.late_ref = bf16[8,3,2,48,1152]{4,3,2,1,0:T(8,128)(2,1)} async-done(((bf16[8,3,2,48,1152]{4,3,2,1,0:T(8,128)(2,1)}), bf16[8,3,2,48,1152]{4,3,2,1,0:T(8,128)(2,1)}, u32[]{:S(2)}, u32[]{:S(2)}) %all-to-all-start.5) | async-done | bytes 5308448 | tf_op jit(solution)/shard_map/all_to_all | solution.py:243
  384.7 30.4 %copy.37.table_ref = bf16[48,384,576]{2,1,0:T(8,128)(2,1)} copy(bf16[48,384,576]{1,2,0:T(8,128)(2,1)} %param.10) | data formatting | bytes 42467328 | tf_op args[4]
  415.1 30.7 %all-to-all-done.2.early_ref = bf16[8,3,2,48,1152]{4,3,2,1,0:T(8,128)(2,1)} async-done(((bf16[8,3,2,48,1152]{4,3,2,1,0:T(8,128)(2,1)}), bf16[8,3,2,48,1152]{4,3,2,1,0:T(8,128)(2,1)}, u32[]{:S(2)}, u32[]{:S(2)}) %all-to-all-start.2) | async-done | bytes 5308448 | tf_op jit(solution)/shard_map/all_to_all | solution.py:243
  445.8 21.7 %shard_map.68 = bf16[3,2,48,32,384]{4,3,2,1,0:T(8,128)(2,1)} custom-call(bf16[8,3,2,48,1152]{4,3,2,1,0:T(8,128)(2,1)} %all-to-all-done.2.early_ref, bf16[8,3,2,48,1152]{4,3,2,1,0:T(8,128)(2,1)} %all-to-all-done.5.late_ref, bf16[48,384,576]{2,1,0:T(8,128)(2,1)} %copy.37.table_ref, bf16[3,2,48,32,384]{4,3,2,1,0:T(8,128)(2,1)} %velocity_ref.1), custom_call_target="tpu_custom_call" | custom-call | flops 4076863488 | bytes 42467328 | tf_op jit(solution)/shard_map/pallas_call | solution.py:191
  467.5 17.7 %reshape.92 = bf16[3,2,48,32,4,96]{5,4,3,2,1,0:T(4,128)(2,1)} reshape(bf16[3,2,48,32,384]{4,3,2,1,0:T(8,128)(2,1)} %shard_map.68) | data formatting | bytes 14155776 | tf_op jit(solution)/shard_map/reshape | solution.py:216
  485.2 9.4 %copy.38 = bf16[3,2,48,32,4,96]{5,3,2,1,0,4:T(8,128)(2,1)} copy(bf16[3,2,48,32,4,96]{5,4,3,2,1,0:T(4,128)(2,1)} %reshape.92) | data formatting | bytes 14155776 | tf_op jit(solution)/shard_map/reshape | solution.py:216
  494.7 11.3 %copy.39 = bf16[4,96,9216]{2,1,0:T(8,128)(2,1)} copy(bf16[4,96,9216]{1,2,0:T(8,128)(2,1)} %bitcast.24) | data formatting | bytes 14155776 | tf_op jit(solution)/shard_map/reshape | solution.py:218
  506.0 5.7 all-to-all-start.6
  515.9 148.6 %all-to-all-done.6 = bf16[4,96,9216]{2,1,0:T(8,128)(2,1)} async-done(((bf16[4,96,9216]{2,1,0:T(8,128)(2,1)}), bf16[4,96,9216]{2,1,0:T(8,128)(2,1)}, u32[]{:S(2)}, u32[]{:S(2)}) %all-to-all-start.6) | async-done | bytes 7077920 | tf_op jit(solution)/shard_map/all_to_all | solution.py:219
  664.5 11.3 %copy.40 = bf16[4,96,9216]{1,2,0:T(8,128)(2,1)} copy(bf16[4,96,9216]{2,1,0:T(8,128)(2,1)} %all-to-all-done.6) | data formatting | bytes 14155776 | tf_op jit(solution)/shard_map/all_to_all | solution.py:219
  675.8 33.0 %copy.42 = bf16[4,96,3,2,48,32]{4,5,0,3,2,1:T(8,128)(2,1)} copy(bf16[4,96,3,2,48,32]{1,5,4,3,2,0:T(8,128)(2,1)} %bitcast.23) | data formatting | bytes 14155776 | tf_op jit(solution)/shard_map/reshape | solution.py:220
  708.8 12.1 %convolution_bitcast_fusion = f32[3,2,48,96,128]{4,2,1,0,3:T(8,128)} fusion(bf16[4,96,3,2,48,32]{4,5,0,3,2,1:T(8,128)(2,1)} %copy.42, bf16[96,128,4,32,1,1]{1,3,2,5,4,0:T(8,128)(2,1)S(1)} %bitcast.25), kind=kOutput, calls=%fused_computation | convolution fusion | flops 905969664 | bytes 24379392 | tf_op jit(solution)/shard_map/qlcpsr,laqr->cpsla/dot_general | solution.py:222
  721.0 18.5 %copy.43 = f32[3,2,48,96,128]{4,3,2,1,0:T(8,128)} copy(f32[3,2,48,96,128]{4,2,1,0,3:T(8,128)} %convolution_bitcast_fusion) | data formatting | bytes 28311552 | tf_op jit(solution)/shard_map/qlcpsr,laqr->cpsla/transpose | solution.py:222
  (14 shorter events, 22.0 us)
Async XLA Ops:
  0.0 30.4 %copy-start.2 = (s32[384]{0:T(512)S(1)}, s32[384]{0:T(512)}, u32[]{:S(2)}) copy-start(s32[384]{0:T(512)} %param.8) | copy-start | bytes 4612
  51.6 66.4 %all-to-all-start.3 = ((bf16[8,3,2,48,1152]{4,3,2,1,0:T(8,128)(2,1)}), bf16[8,3,2,48,1152]{4,3,2,1,0:T(8,128)(2,1)}, u32[]{:S(2)}, u32[]{:S(2)}) async-start(bf16[8,3,2,48,1152]{4,3,2,1,0:T(8,128)(2,1)} %get-tuple-element.11), calls=%async_computation.3 | async-start | bytes 10616832 | tf_op jit(solution)/shard_map/all_to_all | solution.py:243
  118.0 65.9 %copy-start.1 = (bf16[8,3,2,48,1152]{4,3,2,1,0:T(8,128)(2,1)S(1)}, bf16[8,3,2,48,1152]{4,3,2,1,0:T(8,128)(2,1)}, u32[]{:S(2)}) copy-start(bf16[8,3,2,48,1152]{4,3,2,1,0:T(8,128)(2,1)} %get-tuple-element.9) | copy-start | bytes 15925252
  248.2 65.9 %all-to-all-start.1 = ((bf16[8,3,2,48,1152]{4,3,2,1,0:T(8,128)(2,1)}), bf16[8,3,2,48,1152]{4,3,2,1,0:T(8,128)(2,1)}, u32[]{:S(2)}, u32[]{:S(2)}) async-start(bf16[8,3,2,48,1152]{4,3,2,1,0:T(8,128)(2,1)} %get-tuple-element.10), calls=%async_computation.1 | async-start | bytes 10616832 | tf_op jit(solution)/shard_map/all_to_all | solution.py:243
  261.3 2.5 copy-start
  314.2 65.7 %all-to-all-start.5 = ((bf16[8,3,2,48,1152]{4,3,2,1,0:T(8,128)(2,1)}), bf16[8,3,2,48,1152]{4,3,2,1,0:T(8,128)(2,1)}, u32[]{:S(2)}, u32[]{:S(2)}) async-start(bf16[8,3,2,48,1152]{4,3,2,1,0:T(8,128)(2,1)} %shard_map.67), calls=%async_computation.5 | async-start | bytes 10616832 | tf_op jit(solution)/shard_map/all_to_all | solution.py:243
  379.9 65.9 %all-to-all-start.2 = ((bf16[8,3,2,48,1152]{4,3,2,1,0:T(8,128)(2,1)}), bf16[8,3,2,48,1152]{4,3,2,1,0:T(8,128)(2,1)}, u32[]{:S(2)}, u32[]{:S(2)}) async-start(bf16[8,3,2,48,1152]{4,3,2,1,0:T(8,128)(2,1)} %shard_map.66), calls=%async_computation.2 | async-start | bytes 10616832 | tf_op jit(solution)/shard_map/all_to_all | solution.py:243
  506.0 158.5 %all-to-all-start.6 = ((bf16[4,96,9216]{2,1,0:T(8,128)(2,1)}), bf16[4,96,9216]{2,1,0:T(8,128)(2,1)}, u32[]{:S(2)}, u32[]{:S(2)}) async-start(bf16[4,96,9216]{2,1,0:T(8,128)(2,1)} %copy.39), calls=%async_computation.6 | async-start | bytes 14155776 | tf_op jit(solution)/shard_map/all_to_all | solution.py:219

commit v2 on v1

--- a/solution.py
+++ b/solution.py
@@ -16,6 +16,7 @@
 
 LANES = 128
 ROWS = 16
+QUAD = 4
 
 
 time_step = 0.5
@@ -39,13 +40,15 @@
 
 def synth_kernel(scale_ref, spec_ref, table_ref, early_ref, late_ref, turned):
     comps, parts, slots, radii, degrees = spec_ref.shape
-    lat = table_ref.shape[2]
+    lat = table_ref.shape[1]
     half = radii // 2
     rows = comps * parts * half
     first_slot = pl.program_id(0) * slots
     for s in range(slots):
         spec = spec_ref[:, :, s].reshape(2 * rows, degrees)
-        sums = jnp.dot(spec, table_ref[s], preferred_element_type=jnp.float32)
+        sums = lax.dot_general(
+            spec, table_ref[s], (((1,), (1,)), ((), ())), preferred_element_type=jnp.float32
+        )
         sums = (sums * scale_ref[first_slot + s]).reshape(comps * parts, 2, half, lat)
         wide = jnp.concatenate(
             [sums[:, 0].reshape(rows, lat), sums[:, 1].reshape(rows, lat)], axis=1
@@ -66,7 +69,7 @@
 
 def synthesize(spec, table, scale):
     comps, parts, slots, radii, degrees = spec.shape
-    lat = table.shape[2]
+    lat = table.shape[1]
     owners = radii // 4
     shape = jax.ShapeDtypeStruct((owners, comps, parts, slots, 2 * lat), jnp.bfloat16)
     out_spec = pl.BlockSpec((owners, comps, parts, ROWS, 2 * lat), lambda i: (0, 0, 0, i, 0))
@@ -77,7 +80,7 @@
         in_specs=[
             pl.BlockSpec(memory_space=pltpu.SMEM),
             pl.BlockSpec((comps, parts, ROWS, radii, degrees), lambda i: (0, 0, i, 0, 0)),
-            pl.BlockSpec((ROWS, degrees, lat), lambda i: (i, 0, 0)),
+            pl.BlockSpec((ROWS, lat, degrees), lambda i: (i, 0, 0)),
         ],
         out_specs=[out_spec, out_spec],
         out_shape=[shape, shape],
@@ -147,86 +150,144 @@
     )(moving, spinning, across, along)
 
 
-def analyze_kernel(early_ref, late_ref, table_ref, velocity_ref, out_ref, turned):
+def analyze_kernel(h, in_ref, table_ref, velocity_ref, out_ref, turned):
     comps, parts, slots, radii, degrees = velocity_ref.shape
-    lat = table_ref.shape[2]
-    half = radii // 2
-    rows = comps * parts * half
-    owners = half // 2
+    lat = table_ref.shape[1]
+    owners = in_ref.shape[0]
+    rows = comps * parts * owners
+    tiles = 2 * lat // LANES
     for i in range(comps * parts):
-        c, p = i // parts, i % parts
-        for h, in_ref in enumerate((early_ref, late_ref)):
-            for d in range(owners):
-                row = (i * half + h * owners + d) * slots
-                for t in range(2 * lat // LANES):
-                    turned[t, pl.ds(row, slots), :] = in_ref[
-                        d, c, p, :, t * LANES : (t + 1) * LANES
-                    ].astype(jnp.float32)
+        for d in range(owners):
+            row = (i * owners + d) * slots
+            for t in range(tiles):
+                turned[t, pl.ds(row, slots), :] = in_ref[
+                    d, i // parts, i % parts, :, t * LANES : (t + 1) * LANES
+                ].astype(jnp.float32)
+    groups, own = out_ref.shape[0], out_ref.shape[2]
+    for quad in range(slots // QUAD):
+        sides = []
+        for s in range(quad * QUAD, (quad + 1) * QUAD):
+            wide = jnp.concatenate(
+                [turned[t, pl.ds(s, rows, stride=slots), :] for t in range(tiles)], axis=1
+            )
+            pieces = [wide[:, :lat], wide[:, lat:]]
+            pieces = [x.reshape(comps * parts, 1, owners, lat) for x in pieces]
+            left = jnp.concatenate(pieces, axis=1).reshape(2 * rows, lat)
+            terms = jnp.dot(
+                left.astype(jnp.bfloat16), table_ref[s], preferred_element_type=jnp.float32
+            )
+            moving = velocity_ref[:, :, s].astype(jnp.float32)
+            moving = moving.reshape(comps * parts, 2, 2, owners, degrees)[:, :, h]
+            sides.append(moving.reshape(2 * rows, degrees) + time_step * terms)
+        turned_sides = jnp.concatenate(sides, axis=0).T.astype(jnp.bfloat16)
+        for g in range(groups):
+            out_ref[g, quad] = turned_sides[g * own : (g + 1) * own]
+
+
+def analyze(h, back, table, velocity, groups):
+    comps, parts, slots, radii, degrees = velocity.shape
+    lat = table.shape[1]
+    owners = back.shape[0]
+    own = degrees // groups
+    wide = QUAD * comps * parts * 2 * owners
+    rows = comps * parts * owners * ROWS
+    return pl.pallas_call(
+        functools.partial(analyze_kernel, h),
+        grid=(slots // ROWS,),
+        in_specs=[
+            pl.BlockSpec((owners, comps, parts, ROWS, 2 * lat), lambda i: (0, 0, 0, i, 0)),
+            pl.BlockSpec((ROWS, lat, degrees), lambda i: (i, 0, 0)),
+            pl.BlockSpec((comps, parts, ROWS, radii, degrees), lambda i: (0, 0, i, 0, 0)),
+        ],
+        out_specs=pl.BlockSpec((groups, ROWS // QUAD, own, wide), lambda i: (0, i, 0, 0)),
+        out_shape=jax.ShapeDtypeStruct((groups, slots // QUAD, own, wide), jnp.bfloat16),
+        scratch_shapes=[pltpu.VMEM((2 * lat // LANES, rows, LANES), jnp.float32)],
+        compiler_params=pltpu.CompilerParams(vmem_limit_bytes=56 << 20),
+        cost_estimate=pl.CostEstimate(
+            flops=velocity.size * lat,
+            bytes_accessed=2 * (3 * velocity.size + table.size),
+            transcendentals=0,
+        ),
+    )(back, table, velocity)
+
+
+def radial_kernel(early_ref, late_ref, order_ref, operator_ref, out_ref, lines):
+    groups, quads, own, wide = early_ref.shape
+    comps, parts, slots = out_ref.shape[:3]
+    full = out_ref.shape[4]
+    sets = 2 * groups
+    for u in range(wide // LANES):
+        halves = [
+            ref[z, :, :, u * LANES : (u + 1) * LANES].reshape(quads * own, LANES)
+            for z in range(groups)
+            for ref in (early_ref, late_ref)
+        ]
+        packed = jnp.concatenate(halves, axis=1)
+        sorted_lines = jnp.dot(packed, order_ref[...], preferred_element_type=jnp.float32)
+        for g in range(sets):
+            row = (u * sets + g) * quads * own
+            lines[pl.ds(row, quads * own), :] = sorted_lines[:, g * full : (g + 1) * full]
+    count = comps * parts * slots
+    for degree in range(own):
+        left = lines[pl.ds(degree, count, stride=own), :].astype(jnp.bfloat16)
+        lines[pl.ds(degree, count, stride=own), :] = lax.dot_general(
+            left,
+            operator_ref[degree],
+            (((1,), (1,)), ((), ())),
+            preferred_element_type=jnp.float32,
+        )
     for s in range(slots):
-        wide = jnp.concatenate(
-            [
-                turned[t, pl.ds(s, rows, stride=slots), :]
-                for t in range(2 * lat // LANES)
-            ],
-            axis=1,
-        )
-        pieces = [wide[:, :lat], wide[:, lat:]]
-        pieces = [x.astype(jnp.bfloat16).reshape(comps * parts, 1, half, lat) for x in pieces]
-        left = jnp.concatenate(pieces, axis=1).reshape(2 * rows, lat)
-        terms = lax.dot_general(
-            left, table_ref[s], (((1,), (1,)), ((), ())), preferred_element_type=jnp.float32
-        )
-        terms = terms.reshape(comps, parts, radii, degrees)
-        sides = velocity_ref[:, :, s].astype(jnp.float32) + time_step * terms
-        out_ref[:, :, s] = sides.astype(jnp.bfloat16)
-
-
-def analyze(early, late, table, velocity):
-    comps, parts, slots, radii, degrees = velocity.shape
-    lat = table.shape[2]
-    owners = radii // 4
-    block = pl.BlockSpec((owners, comps, parts, ROWS, 2 * lat), lambda i: (0, 0, 0, i, 0))
-    spec_block = pl.BlockSpec((comps, parts, ROWS, radii, degrees), lambda i: (0, 0, i, 0, 0))
-    rows = comps * parts * radii // 2 * ROWS
+        for i in range(comps * parts):
+            row = ((s % QUAD * comps * parts + i) * quads + s // QUAD) * own
+            out_ref[i // parts, i % parts, s] = lines[pl.ds(row, own), :]
+
+
+def radial_order(groups, owners, full):
+    sets = LANES // (2 * owners)
+    lane = jnp.arange(2 * groups * LANES, dtype=jnp.int32)
+    d, k = lane % owners, lane // owners % 2
+    g = lane // (2 * owners) % sets
+    h, z = lane // LANES % 2, lane // (2 * LANES)
+    target = g * full + ((z * 2 + k) * 2 + h) * owners + d
+    columns = jnp.arange(sets * full, dtype=jnp.int32)
+    return (target[:, None] == columns[None, :]).astype(jnp.bfloat16)
+
+
+def radial_solve(early, late, operators, comps, parts, slots, owners):
+    groups, quads, own, wide = early.shape
+    full = operators.shape[1]
+    order = radial_order(groups, owners, full)
+    block = pl.BlockSpec((groups, ROWS // QUAD, own, wide), lambda i: (0, i, 0, 0))
     return pl.pallas_call(
-        analyze_kernel,
+        radial_kernel,
         grid=(slots // ROWS,),
         in_specs=[
             block,
             block,
-            pl.BlockSpec((ROWS, degrees, lat), lambda i: (i, 0, 0)),
-            spec_block,
+            pl.BlockSpec(order.shape, lambda i: (0, 0)),
+            pl.BlockSpec(operators.shape, lambda i: (0, 0, 0)),
         ],
-        out_specs=spec_block,
-        out_shape=jax.ShapeDtypeStruct(velocity.shape, jnp.bfloat16),
-        scratch_shapes=[pltpu.VMEM((2 * lat // LANES, rows, LANES), jnp.float32)],
+        out_specs=pl.BlockSpec((comps, parts, ROWS, own, full), lambda i: (0, 0, i, 0, 0)),
+        out_shape=jax.ShapeDtypeStruct((comps, parts, slots, own, full), jnp.float32),
+        scratch_shapes=[pltpu.VMEM((comps * parts * ROWS * own, LANES), jnp.float32)],
         compiler_params=pltpu.CompilerParams(vmem_limit_bytes=56 << 20),
         cost_estimate=pl.CostEstimate(
-            flops=2 * velocity.size * lat,
-            bytes_accessed=2 * (3 * velocity.size + table.size),
+            flops=4 * early.size * order.shape[0],
+            bytes_accessed=12 * early.size,
             transcendentals=0,
         ),
-    )(early, late, table, velocity)
-
-
-def radial_solve(right_side, inverse_operators):
-    comps, parts, slots, radii, degrees = right_side.shape
-    own, full = inverse_operators.shape[:2]
-    groups = full // radii
-    split = right_side.reshape(comps, parts, slots, radii, groups, own)
-    split = jnp.transpose(split, (4, 5, 0, 1, 2, 3))
-    split = split.reshape(groups, own, comps * parts * slots * radii)
-    pieces = lax.all_to_all(split, "row", split_axis=0, concat_axis=0, tiled=True)
-    columns = pieces.reshape(groups, own, comps, parts, slots, radii)
-    operators = inverse_operators.astype(jnp.bfloat16).reshape(own, full, groups, radii)
-    return jnp.einsum(
-        "qlcpsr,laqr->cpsla", columns, operators, preferred_element_type=jnp.float32
-    )
-
-
-def fits(velocity, legendre_bf, owners):
+    )(early, late, order, operators)
+
+
+def fits(velocity, legendre_bf, owners, groups):
+    comps, parts, slots, radii, degrees = velocity.shape
     return (
-        velocity.shape[3] == 4 * owners
+        groups * radii == LANES
+        and LANES % (2 * owners) == 0
+        and owners % 8 == 0
+        and QUAD * comps * parts * 2 * owners % LANES == 0
+        and degrees % (groups * ROWS) == 0
+        and velocity.shape[3] == 4 * owners
         and velocity.shape[3] % (2 * ROWS) == 0
         and velocity.shape[2] % ROWS == 0
         and (2 * legendre_bf.shape[2]) % (3 * LANES) == 0
@@ -242,8 +303,10 @@
     def exchange(x):
         return lax.all_to_all(x, "ma", split_axis=0, concat_axis=0, tiled=True)
 
-    move_early, move_late = synthesize(velocity, legendre_bf, scale)
-    spin_early, spin_late = synthesize(vorticity, legendre_bf, scale)
+    legendre = jnp.transpose(legendre_bf, (0, 2, 1))
+    weights = jnp.transpose(weighted, (0, 2, 1))
+    move_early, move_late = synthesize(velocity, legendre, scale)
+    spin_early, spin_late = synthesize(vorticity, legendre, scale)
     move_early, spin_early = exchange(move_early), exchange(spin_early)
     move_late, spin_late = exchange(move_late), exchange(spin_late)
     table = longitude_table(order_table).reshape(2, owners, slots, NLON)
@@ -251,12 +314,23 @@
     across = jnp.transpose(along)
     early = exchange(through_grid(move_early, spin_early, across, along, NL / NLON))
     late = exchange(through_grid(move_late, spin_late, across, along, NL / NLON))
-    right_side = analyze(early, late, weighted, velocity)
-    return radial_solve(right_side, inverse_operators)
+    groups = lax.axis_size("row")
+    sides = [
+        lax.all_to_all(
+            analyze(h, back, weights, velocity, groups),
+            "row",
+            split_axis=0,
+            concat_axis=0,
+            tiled=True,
+        )
+        for h, back in enumerate((early, late))
+    ]
+    operators = inverse_operators.astype(jnp.bfloat16)
+    return radial_solve(*sides, operators, *velocity.shape[:3], owners)
 
 
 def per_device(velocity, vorticity, order_table, legendre_bf, weighted, inverse_operators):
-    if fits(velocity, legendre_bf, lax.axis_size("ma")):
+    if fits(velocity, legendre_bf, lax.axis_size("ma"), lax.axis_size("row")):
         return by_radius(
             velocity, vorticity, order_table, legendre_bf, weighted, inverse_operators
         )

time: 750 us -> 617 us (0.82); the launches traced: 740 us -> 615 us
  local copies, waits for them, and re-layouts: 169 us -> 2.62 us
  Pallas kernels: 120 us -> 164 us
  matrix products: 12.1 us -> 0 us
  other arithmetic: 8.81 us -> 16.4 us
    reshape x4 -> x0, local copies, waits for them, and re-layouts: 71.6 us -> none  [the longest x1 33 us: radial_solve(): columns = pieces.reshape(groups, own, comps, parts, slots, radii)]
    unnamed x9 -> x10, local copies, waits for them, and re-layouts: 65 us -> 0.02 us
    pallas_call x1 -> x3, Pallas kernels: 21.7 us -> 64.7 us  [the longest x1 33.7 us: radial_solve(): pl.pallas_call(radial_kernel, grid=(slots // ROWS,), in_specs=[block, blo...]
    transpose x1 -> x0, local copies, waits for them, and re-layouts: 18.5 us -> none  [radial_solve(): jnp.einsum('qlcpsr,laqr->cpsla', columns, operators, preferred_element_ty...]
    all_to_all x1 -> x2, waiting for transfers between devices: 149 us -> 132 us  [by_radius(): lax.all_to_all(analyze(h, back, weights, velocity, groups), 'row', split_...]
    all_to_all x4, waiting for transfers between devices: 125 us -> 139 us  [exchange(): return lax.all_to_all(x, 'ma', split_axis=0, concat_axis=0, tiled=True)]
    dot_general x1 -> x0, matrix products: 12.1 us -> none  [radial_solve(): jnp.einsum('qlcpsr,laqr->cpsla', columns, operators, preferred_element_ty...]
    all_to_all x1 -> x0, local copies, waits for them, and re-layouts: 11.3 us -> none  [radial_solve(): lax.all_to_all(split, 'row', split_axis=0, concat_axis=0, tiled=True)]
  transfers between devices with their start and end apart: 5 -> 6, of which waited for: 5 -> 6; matrix products, arithmetic and copies ran while one was open for 6% -> 3% of each run, Pallas kernels for 11% -> 18%
where the time goes in v2:
time: 617 us; the launch traced here: 615 us
  waiting for transfers between devices  271 us (44%)
  Pallas kernels  164 us (27%)
  blocking collectives  130 us (21%)
  starting transfers between devices  30.4 us (5%)
  other arithmetic  16.4 us (3%)
    all_to_all x4, waiting for transfers between devices, exchange(): return lax.all_to_all(x, 'ma', split_axis=0, concat_axis=0, tiled=True)  139 us
    all_to_all x2, waiting for transfers between devices, by_radius(): lax.all_to_all(analyze(h, back, weights, velocity, groups), 'row', split_...  132 us
    all_to_all x2, blocking collectives, exchange(): return lax.all_to_all(x, 'ma', split_axis=0, concat_axis=0, tiled=True)  130 us
    pallas_call x2, Pallas kernels, through_grid(): pl.pallas_call(functools.partial(grid_kernel, scale), grid=(columns // wi...  57.5 us
    pallas_call x2, Pallas kernels, synthesize(): pl.pallas_call(synth_kernel, grid=(slots // ROWS,), in_specs=[pl.BlockSpe...  41.9 us
    pallas_call x1, Pallas kernels, radial_solve(): pl.pallas_call(radial_kernel, grid=(slots // ROWS,), in_specs=[block, blo...  33.7 us
    pallas_call x2, Pallas kernels, analyze(): pl.pallas_call(functools.partial(analyze_kernel, h), grid=(slots // ROWS,...  31 us
    all_to_all x4, starting transfers between devices, exchange(): return lax.all_to_all(x, 'ma', split_axis=0, concat_axis=0, tiled=True)  19.7 us
  transfers between devices with their start and end apart: 6, of which 6 were waited for; matrix products, arithmetic and copies ran while one was open for 3% of the time, Pallas kernels for 18%

profile of v2, /device:TPU:0, one launch (start us, length us, event | category | flops | bytes accessed | tf_op | source)
XLA Modules:
  0.0 615.2 jit_solution(14267445422870667466)
XLA Ops:
  1.3 20.9 %shard_map.64 = (bf16[8,3,2,48,1152]{4,3,2,1,0:T(8,128)(2,1)}, bf16[8,3,2,48,1152]{4,3,2,1,0:T(8,128)(2,1)}) custom-call(f32[48]{0:T(128)} %fusion.30.scale_ref, bf16[3,2,48,32,384]{4,3,2,1,0:T(8,128)(2,1)} %velocity_ref.3, bf16[48,576,384]{2,1,0:T(8,128)(2,1)} %bitcast.9), custom_call_target="tpu_custom_call" | custom-call | flops 4076863488 | bytes 38928384 | tf_op jit(solution)/shard_map/pallas_call | solution.py:77
  22.3 5.2 all-to-all-start.4
  27.5 20.9 %shard_map.65 = (bf16[8,3,2,48,1152]{4,3,2,1,0:T(8,128)(2,1)}, bf16[8,3,2,48,1152]{4,3,2,1,0:T(8,128)(2,1)}) custom-call(f32[48]{0:T(128)} %fusion.30.scale_ref, bf16[3,2,48,32,384]{4,3,2,1,0:T(8,128)(2,1)} %spec_ref.3, bf16[48,576,384]{2,1,0:T(8,128)(2,1)} %bitcast.10), custom_call_target="tpu_custom_call" | custom-call | flops 4076863488 | bytes 38928384 | tf_op jit(solution)/shard_map/pallas_call | solution.py:77
  48.4 40.3 %all-to-all-done.4.move_ref = bf16[8,3,2,48,1152]{4,3,2,1,0:T(8,128)(2,1)} async-done(((bf16[8,3,2,48,1152]{4,3,2,1,0:T(8,128)(2,1)}), bf16[8,3,2,48,1152]{4,3,2,1,0:T(8,128)(2,1)}, u32[]{:S(2)}, u32[]{:S(2)}) %all-to-all-start.4) | async-done | bytes 5308448 | tf_op jit(solution)/shard_map/all_to_all | solution.py:304
  88.7 65.9 %all_to_all.40.spin_ref = bf16[8,3,2,48,1152]{4,3,2,1,0:T(8,128)(2,1)} all-to-all(bf16[8,3,2,48,1152]{4,3,2,1,0:T(8,128)(2,1)} %get-tuple-element.12), channel_id=1, replica_groups=mesh['ma'=8,'row'=4] {'ma'}, dimensions={0} | all-to-all | bytes 10616832 | tf_op jit(solution)/shard_map/all_to_all | solution.py:304
  154.6 64.3 %all_to_all.41.move_ref = bf16[8,3,2,48,1152]{4,3,2,1,0:T(8,128)(2,1)} all-to-all(bf16[8,3,2,48,1152]{4,3,2,1,0:T(8,128)(2,1)S(1)} %bitcast.15), channel_id=1, replica_groups=mesh['ma'=8,'row'=4] {'ma'}, dimensions={0} | all-to-all | bytes 10616832 | tf_op jit(solution)/shard_map/all_to_all | solution.py:304
  218.9 5.0 all-to-all-start.1
  224.0 8.0 %cosine_convert_fusion = (bf16[1,8,48,1152]{3,2,0,1:T(8,128)(2,1)S(1)}, bf16[1,8,48,1152]{3,2,0,1:T(8,128)(2,1)S(1)}) fusion(s32[8,48]{1,0:T(8,128)S(1)} %mul.83), kind=kLoop, calls=%fused_computation.7 | loop fusion | flops 5308416 | bytes 1771008 | tf_op jit(solution)/shard_map/convert
  232.2 2.5 copy.7.across_ref
  234.7 28.8 %shard_map.68 = bf16[8,3,2,48,1152]{4,3,2,1,0:T(8,128)(2,1)} custom-call(bf16[8,3,2,48,1152]{4,3,2,1,0:T(8,128)(2,1)} %all-to-all-done.4.move_ref, bf16[8,3,2,48,1152]{4,3,2,1,0:T(8,128)(2,1)} %all_to_all.40.spin_ref, bf16[1152,768]{1,0:T(8,128)(2,1)} %copy.7.across_ref, bf16[768,1152]{1,0:T(8,128)(2,1)} %bitcast.12), custom_call_target="tpu_custom_call" | custom-call | flops 18345885696 | bytes 15925248 | tf_op jit(solution)/shard_map/pallas_call | solution.py:129
  263.5 21.3 %all-to-all-done.1.spin_ref = bf16[8,3,2,48,1152]{4,3,2,1,0:T(8,128)(2,1)} async-done(((bf16[8,3,2,48,1152]{4,3,2,1,0:T(8,128)(2,1)}), bf16[8,3,2,48,1152]{4,3,2,1,0:T(8,128)(2,1)}, u32[]{:S(2)}, u32[]{:S(2)}) %all-to-all-start.1) | async-done | bytes 5308448 | tf_op jit(solution)/shard_map/all_to_all | solution.py:304
  284.8 4.9 all-to-all-start.6
  289.7 28.7 %shard_map.66 = bf16[8,3,2,48,1152]{4,3,2,1,0:T(8,128)(2,1)} custom-call(bf16[8,3,2,48,1152]{4,3,2,1,0:T(8,128)(2,1)} %all_to_all.41.move_ref, bf16[8,3,2,48,1152]{4,3,2,1,0:T(8,128)(2,1)} %all-to-all-done.1.spin_ref, bf16[1152,768]{1,0:T(8,128)(2,1)} %copy.7.across_ref, bf16[768,1152]{1,0:T(8,128)(2,1)} %bitcast.13), custom_call_target="tpu_custom_call" | custom-call | flops 18345885696 | bytes 15925248 | tf_op jit(solution)/shard_map/pallas_call | solution.py:129
  318.4 32.1 %all-to-all-done.6.in_ref = bf16[8,3,2,48,1152]{4,3,2,1,0:T(8,128)(2,1)} async-done(((bf16[8,3,2,48,1152]{4,3,2,1,0:T(8,128)(2,1)}), bf16[8,3,2,48,1152]{4,3,2,1,0:T(8,128)(2,1)}, u32[]{:S(2)}, u32[]{:S(2)}) %all-to-all-start.6) | async-done | bytes 5308448 | tf_op jit(solution)/shard_map/all_to_all | solution.py:304
  350.5 4.7 all-to-all-start.2
  355.2 15.6 %shard_map.69 = bf16[4,12,96,384]{3,2,1,0:T(8,128)(2,1)} custom-call(bf16[8,3,2,48,1152]{4,3,2,1,0:T(8,128)(2,1)} %all-to-all-done.6.in_ref, bf16[48,576,384]{2,1,0:T(8,128)(2,1)} %bitcast.7, bf16[3,2,48,32,384]{4,3,2,1,0:T(8,128)(2,1)} %velocity_ref.3), custom_call_target="tpu_custom_call" | custom-call | flops 2038431744 | bytes 42467328 | tf_op jit(solution)/shard_map/pallas_call | solution.py:194
  370.8 45.5 %all-to-all-done.2.in_ref = bf16[8,3,2,48,1152]{4,3,2,1,0:T(8,128)(2,1)} async-done(((bf16[8,3,2,48,1152]{4,3,2,1,0:T(8,128)(2,1)}), bf16[8,3,2,48,1152]{4,3,2,1,0:T(8,128)(2,1)}, u32[]{:S(2)}, u32[]{:S(2)}) %all-to-all-start.2) | async-done | bytes 5308448 | tf_op jit(solution)/shard_map/all_to_all | solution.py:304
  416.3 5.7 all-to-all-start.7
  421.9 15.5 %shard_map.67 = bf16[4,12,96,384]{3,2,1,0:T(8,128)(2,1)} custom-call(bf16[8,3,2,48,1152]{4,3,2,1,0:T(8,128)(2,1)} %all-to-all-done.2.in_ref, bf16[48,576,384]{2,1,0:T(8,128)(2,1)} %bitcast.8, bf16[3,2,48,32,384]{4,3,2,1,0:T(8,128)(2,1)} %velocity_ref.3), custom_call_target="tpu_custom_call" | custom-call | flops 2038431744 | bytes 42467328 | tf_op jit(solution)/shard_map/pallas_call | solution.py:194
  437.4 60.7 %all-to-all-done.7.late_ref = bf16[4,12,96,384]{3,2,1,0:T(8,128)(2,1)S(1)} async-done(((bf16[4,12,96,384]{3,2,1,0:T(8,128)(2,1)}), bf16[4,12,96,384]{3,2,1,0:T(8,128)(2,1)S(1)}, u32[]{:S(2)}, u32[]{:S(2)}) %all-to-all-start.7) | async-done | bytes 3538976 | tf_op jit(solution)/shard_map/all_to_all | solution.py:319
  498.1 5.0 all-to-all-start.3
  503.1 5.2 convert_element_type.26.operator_ref
  510.0 71.5 %all-to-all-done.3.early_ref = bf16[4,12,96,384]{3,2,1,0:T(8,128)(2,1)} async-done(((bf16[4,12,96,384]{3,2,1,0:T(8,128)(2,1)}), bf16[4,12,96,384]{3,2,1,0:T(8,128)(2,1)}, u32[]{:S(2)}, u32[]{:S(2)}) %all-to-all-start.3) | async-done | bytes 3538976 | tf_op jit(solution)/shard_map/all_to_all | solution.py:319
  581.4 33.7 %shard_map.70 = f32[3,2,48,96,128]{4,3,2,1,0:T(8,128)} custom-call(bf16[4,12,96,384]{3,2,1,0:T(8,128)(2,1)} %all-to-all-done.3.early_ref, bf16[4,12,96,384]{3,2,1,0:T(8,128)(2,1)} %copy-done.1, bf16[1024,1024]{1,0:T(8,128)(2,1)} %fusion.order_ref, bf16[96,128,128]{2,1,0:T(8,128)(2,1)} %convert_element_type.26.operator_ref), custom_call_target="tpu_custom_call" | custom-call | flops 7247757312 | bytes 21233664 | tf_op jit(solution)/shard_map/pallas_call | solution.py:261
  (16 shorter events, 3.3 us)
Async XLA Ops:
  22.3 66.4 %all-to-all-start.4 = ((bf16[8,3,2,48,1152]{4,3,2,1,0:T(8,128)(2,1)}), bf16[8,3,2,48,1152]{4,3,2,1,0:T(8,128)(2,1)}, u32[]{:S(2)}, u32[]{:S(2)}) async-start(bf16[8,3,2,48,1152]{4,3,2,1,0:T(8,128)(2,1)} %get-tuple-element.11), calls=%async_computation.4 | async-start | bytes 10616832 | tf_op jit(solution)/shard_map/all_to_all | solution.py:304
  88.7 65.9 %slice-start = ((s8[5308416]{0:T(1024)(128)(4,1)}), s8[4194304]{0:T(1024)(128)(4,1)S(1)}, s32[]{:S(2)}) async-start(s8[5308416]{0:T(1024)(128)(4,1)} %bitcast.14), calls=%async_computation.8 | async-start | bytes 8388608
  88.7 65.9 %slice-start.1 = ((s8[5308416]{0:T(1024)(128)(4,1)}), s8[1114112]{0:T(1024)(128)(4,1)S(1)}, s32[]{:S(2)}) async-start(s8[5308416]{0:T(1024)(128)(4,1)} %bitcast.14), calls=%async_computation.9 | async-start | bytes 2228224
  218.9 5.0 copy-start.2
  218.9 65.9 %all-to-all-start.1 = ((bf16[8,3,2,48,1152]{4,3,2,1,0:T(8,128)(2,1)}), bf16[8,3,2,48,1152]{4,3,2,1,0:T(8,128)(2,1)}, u32[]{:S(2)}, u32[]{:S(2)}) async-start(bf16[8,3,2,48,1152]{4,3,2,1,0:T(8,128)(2,1)} %get-tuple-element.10), calls=%async_computation.1 | async-start | bytes 10616832 | tf_op jit(solution)/shard_map/all_to_all | solution.py:304
  232.2 2.5 copy-start
  284.8 65.7 %all-to-all-start.6 = ((bf16[8,3,2,48,1152]{4,3,2,1,0:T(8,128)(2,1)}), bf16[8,3,2,48,1152]{4,3,2,1,0:T(8,128)(2,1)}, u32[]{:S(2)}, u32[]{:S(2)}) async-start(bf16[8,3,2,48,1152]{4,3,2,1,0:T(8,128)(2,1)} %shard_map.68), calls=%async_computation.6 | async-start | bytes 10616832 | tf_op jit(solution)/shard_map/all_to_all | solution.py:304
  350.5 65.7 %all-to-all-start.2 = ((bf16[8,3,2,48,1152]{4,3,2,1,0:T(8,128)(2,1)}), bf16[8,3,2,48,1152]{4,3,2,1,0:T(8,128)(2,1)}, u32[]{:S(2)}, u32[]{:S(2)}) async-start(bf16[8,3,2,48,1152]{4,3,2,1,0:T(8,128)(2,1)} %shard_map.66), calls=%async_computation.2 | async-start | bytes 10616832 | tf_op jit(solution)/shard_map/all_to_all | solution.py:304
  416.3 81.8 %all-to-all-start.7 = ((bf16[4,12,96,384]{3,2,1,0:T(8,128)(2,1)}), bf16[4,12,96,384]{3,2,1,0:T(8,128)(2,1)S(1)}, u32[]{:S(2)}, u32[]{:S(2)}) async-start(bf16[4,12,96,384]{3,2,1,0:T(8,128)(2,1)} %shard_map.69), calls=%async_computation.7 | async-start | bytes 7077888 | tf_op jit(solution)/shard_map/all_to_all | solution.py:319
  498.1 10.2 %copy-start.1 = (bf16[4,12,96,384]{3,2,1,0:T(8,128)(2,1)}, bf16[4,12,96,384]{3,2,1,0:T(8,128)(2,1)S(1)}, u32[]{:S(2)}) copy-start(bf16[4,12,96,384]{3,2,1,0:T(8,128)(2,1)S(1)} %all-to-all-done.7.late_ref) | copy-start | bytes 10616836
  498.1 83.4 %all-to-all-start.3 = ((bf16[4,12,96,384]{3,2,1,0:T(8,128)(2,1)}), bf16[4,12,96,384]{3,2,1,0:T(8,128)(2,1)}, u32[]{:S(2)}, u32[]{:S(2)}) async-start(bf16[4,12,96,384]{3,2,1,0:T(8,128)(2,1)} %shard_map.67), calls=%async_computation.3 | async-start | bytes 7077888 | tf_op jit(solution)/shard_map/all_to_all | solution.py:319

commit v3 on v2

--- a/solution.py
+++ b/solution.py
@@ -211,18 +211,20 @@
     )(back, table, velocity)
 
 
-def radial_kernel(early_ref, late_ref, order_ref, operator_ref, out_ref, lines):
-    groups, quads, own, wide = early_ref.shape
+def radial_kernel(*refs):
+    *piece_refs, order_ref, operator_ref, out_ref, lines, solved = refs
+    quads, own, wide = piece_refs[0].shape
     comps, parts, slots = out_ref.shape[:3]
     full = out_ref.shape[4]
-    sets = 2 * groups
+    sets = len(piece_refs)
     for u in range(wide // LANES):
-        halves = [
-            ref[z, :, :, u * LANES : (u + 1) * LANES].reshape(quads * own, LANES)
-            for z in range(groups)
-            for ref in (early_ref, late_ref)
-        ]
-        packed = jnp.concatenate(halves, axis=1)
+        packed = jnp.concatenate(
+            [
+                ref[:, :, u * LANES : (u + 1) * LANES].reshape(quads * own, LANES)
+                for ref in piece_refs
+            ],
+            axis=1,
+        )
         sorted_lines = jnp.dot(packed, order_ref[...], preferred_element_type=jnp.float32)
         for g in range(sets):
             row = (u * sets + g) * quads * own
@@ -230,53 +232,62 @@
     count = comps * parts * slots
     for degree in range(own):
         left = lines[pl.ds(degree, count, stride=own), :].astype(jnp.bfloat16)
-        lines[pl.ds(degree, count, stride=own), :] = lax.dot_general(
-            left,
-            operator_ref[degree],
-            (((1,), (1,)), ((), ())),
-            preferred_element_type=jnp.float32,
+        solved[pl.ds(degree, count, stride=own), :] = jnp.dot(
+            left, operator_ref[degree], preferred_element_type=jnp.float32
         )
     for s in range(slots):
         for i in range(comps * parts):
             row = ((s % QUAD * comps * parts + i) * quads + s // QUAD) * own
-            out_ref[i // parts, i % parts, s] = lines[pl.ds(row, own), :]
-
-
-def radial_order(groups, owners, full):
+            out_ref[i // parts, i % parts, s] = solved[pl.ds(row, own), :]
+
+
+def radial_order(groups, owners, full, me):
     sets = LANES // (2 * owners)
     lane = jnp.arange(2 * groups * LANES, dtype=jnp.int32)
     d, k = lane % owners, lane // owners % 2
     g = lane // (2 * owners) % sets
-    h, z = lane // LANES % 2, lane // (2 * LANES)
+    step, h = lane // LANES % groups, lane // (LANES * groups)
+    z = (me - step + groups) % groups
     target = g * full + ((z * 2 + k) * 2 + h) * owners + d
     columns = jnp.arange(sets * full, dtype=jnp.int32)
     return (target[:, None] == columns[None, :]).astype(jnp.bfloat16)
 
 
-def radial_solve(early, late, operators, comps, parts, slots, owners):
-    groups, quads, own, wide = early.shape
+def radial_solve(pieces, order, operators, comps, parts, slots):
+    quads, own, wide = pieces[0].shape
     full = operators.shape[1]
-    order = radial_order(groups, owners, full)
-    block = pl.BlockSpec((groups, ROWS // QUAD, own, wide), lambda i: (0, i, 0, 0))
+    block = pl.BlockSpec((quads, 2 * ROWS, wide), lambda i: (0, i, 0))
+    scratch = pltpu.VMEM((comps * parts * slots * 2 * ROWS, LANES), jnp.float32)
     return pl.pallas_call(
         radial_kernel,
-        grid=(slots // ROWS,),
-        in_specs=[
-            block,
-            block,
+        grid=(own // (2 * ROWS),),
+        in_specs=[block] * len(pieces)
+        + [
             pl.BlockSpec(order.shape, lambda i: (0, 0)),
-            pl.BlockSpec(operators.shape, lambda i: (0, 0, 0)),
+            pl.BlockSpec((2 * ROWS, full, full), lambda i: (i, 0, 0)),
         ],
-        out_specs=pl.BlockSpec((comps, parts, ROWS, own, full), lambda i: (0, 0, i, 0, 0)),
+        out_specs=pl.BlockSpec((comps, parts, slots, 2 * ROWS, full), lambda i: (0, 0, 0, i, 0)),
         out_shape=jax.ShapeDtypeStruct((comps, parts, slots, own, full), jnp.float32),
-        scratch_shapes=[pltpu.VMEM((comps * parts * ROWS * own, LANES), jnp.float32)],
+        scratch_shapes=[scratch, scratch],
         compiler_params=pltpu.CompilerParams(vmem_limit_bytes=56 << 20),
         cost_estimate=pl.CostEstimate(
-            flops=4 * early.size * order.shape[0],
-            bytes_accessed=12 * early.size,
+            flops=2 * len(pieces) * pieces[0].size * order.shape[0],
+            bytes_accessed=6 * len(pieces) * pieces[0].size,
             transcendentals=0,
         ),
-    )(early, late, order, operators)
+    )(*pieces, order, operators)
+
+
+def share_degrees(sides, groups):
+    me = lax.axis_index("row")
+    pieces = []
+    for step in range(groups):
+        block = lax.dynamic_index_in_dim(sides, (me + step) % groups, keepdims=False)
+        if step:
+            places = [(i, (i + step) % groups) for i in range(groups)]
+            block = lax.ppermute(block, "row", places)
+        pieces.append(block)
+    return pieces
 
 
 def fits(velocity, legendre_bf, owners, groups):
@@ -286,7 +297,7 @@
         and LANES % (2 * owners) == 0
         and owners % 8 == 0
         and QUAD * comps * parts * 2 * owners % LANES == 0
-        and degrees % (groups * ROWS) == 0
+        and degrees % (groups * 2 * ROWS) == 0
         and velocity.shape[3] == 4 * owners
         and velocity.shape[3] % (2 * ROWS) == 0
         and velocity.shape[2] % ROWS == 0
@@ -315,18 +326,12 @@
     early = exchange(through_grid(move_early, spin_early, across, along, NL / NLON))
     late = exchange(through_grid(move_late, spin_late, across, along, NL / NLON))
     groups = lax.axis_size("row")
-    sides = [
-        lax.all_to_all(
-            analyze(h, back, weights, velocity, groups),
-            "row",
-            split_axis=0,
-            concat_axis=0,
-            tiled=True,
-        )
-        for h, back in enumerate((early, late))
-    ]
-    operators = inverse_operators.astype(jnp.bfloat16)
-    return radial_solve(*sides, operators, *velocity.shape[:3], owners)
+    pieces = []
+    for h, back in enumerate((early, late)):
+        pieces += share_degrees(analyze(h, back, weights, velocity, groups), groups)
+    order = radial_order(groups, owners, groups * velocity.shape[3], lax.axis_index("row"))
+    operators = jnp.transpose(inverse_operators, (0, 2, 1)).astype(jnp.bfloat16)
+    return radial_solve(pieces, order, operators, *velocity.shape[:3])
 
 
 def per_device(velocity, vorticity, order_table, legendre_bf, weighted, inverse_operators):

time: 617 us -> 569 us (0.922)
  the two profiles are of different devices: /device:TPU:0 before, /device:TPU:11 now
where the time goes in v3:
time: 569 us; the launch traced here: 563 us
  waiting for transfers between devices  211 us (37%)
  Pallas kernels  162 us (28%)
  blocking collectives  130 us (23%)
  starting transfers between devices  32.3 us (6%)
  local copies, waits for them, and re-layouts  15.8 us (3%)
  other arithmetic  11.3 us (2%)
    all_to_all x2, blocking collectives, exchange(): return lax.all_to_all(x, 'ma', split_axis=0, concat_axis=0, tiled=True)  130 us
    all_to_all x4, waiting for transfers between devices, exchange(): return lax.all_to_all(x, 'ma', split_axis=0, concat_axis=0, tiled=True)  126 us
    ppermute x6, waiting for transfers between devices, share_degrees(): block = lax.ppermute(block, 'row', places)  84.3 us
    pallas_call x2, Pallas kernels, through_grid(): pl.pallas_call(functools.partial(grid_kernel, scale), grid=(columns // wi...  57.5 us
    pallas_call x2, Pallas kernels, synthesize(): pl.pallas_call(synth_kernel, grid=(slots // ROWS,), in_specs=[pl.BlockSpe...  41.9 us
    pallas_call x1, Pallas kernels, radial_solve(): pl.pallas_call(radial_kernel, grid=(own // (2 * ROWS),), in_specs=[block]...  31.9 us
    pallas_call x2, Pallas kernels, analyze(): pl.pallas_call(functools.partial(analyze_kernel, h), grid=(slots // ROWS,...  30.9 us
    all_to_all x4, starting transfers between devices, exchange(): return lax.all_to_all(x, 'ma', split_axis=0, concat_axis=0, tiled=True)  24.6 us
  transfers between devices with their start and end apart: 10, of which 9 were waited for; matrix products, arithmetic and copies ran while one was open for 4% of the time, Pallas kernels for 19%

profile of v3, /device:TPU:11, one launch (start us, length us, event | category | flops | bytes accessed | tf_op | source)
XLA Modules:
  0.0 562.9 jit_solution(4838014190341655205)
XLA Ops:
  1.3 20.9 %shard_map.64 = (bf16[8,3,2,48,1152]{4,3,2,1,0:T(8,128)(2,1)}, bf16[8,3,2,48,1152]{4,3,2,1,0:T(8,128)(2,1)}) custom-call(f32[48]{0:T(128)} %fusion.31.scale_ref, bf16[3,2,48,32,384]{4,3,2,1,0:T(8,128)(2,1)} %velocity_ref.3, bf16[48,576,384]{2,1,0:T(8,128)(2,1)} %bitcast.28), custom_call_target="tpu_custom_call" | custom-call | flops 4076863488 | bytes 38928384 | tf_op jit(solution)/shard_map/pallas_call | solution.py:77
  22.3 5.4 all-to-all-start
  27.7 21.0 %shard_map.65 = (bf16[8,3,2,48,1152]{4,3,2,1,0:T(8,128)(2,1)}, bf16[8,3,2,48,1152]{4,3,2,1,0:T(8,128)(2,1)}) custom-call(f32[48]{0:T(128)} %fusion.31.scale_ref, bf16[3,2,48,32,384]{4,3,2,1,0:T(8,128)(2,1)} %spec_ref.3, bf16[48,576,384]{2,1,0:T(8,128)(2,1)} %bitcast.29), custom_call_target="tpu_custom_call" | custom-call | flops 4076863488 | bytes 38928384 | tf_op jit(solution)/shard_map/pallas_call | solution.py:77
  48.6 38.6 %all-to-all-done.move_ref = bf16[8,3,2,48,1152]{4,3,2,1,0:T(8,128)(2,1)} async-done(((bf16[8,3,2,48,1152]{4,3,2,1,0:T(8,128)(2,1)}), bf16[8,3,2,48,1152]{4,3,2,1,0:T(8,128)(2,1)}, u32[]{:S(2)}, u32[]{:S(2)}) %all-to-all-start) | async-done | bytes 5308448 | tf_op jit(solution)/shard_map/all_to_all | solution.py:315
  87.3 65.9 %all_to_all.30.spin_ref = bf16[8,3,2,48,1152]{4,3,2,1,0:T(8,128)(2,1)} all-to-all(bf16[8,3,2,48,1152]{4,3,2,1,0:T(8,128)(2,1)} %get-tuple-element.10), channel_id=1, replica_groups=mesh['ma'=8,'row'=4] {'ma'}, dimensions={0} | all-to-all | bytes 10616832 | tf_op jit(solution)/shard_map/all_to_all | solution.py:315
  153.1 64.3 %all_to_all.31.move_ref = bf16[8,3,2,48,1152]{4,3,2,1,0:T(8,128)(2,1)} all-to-all(bf16[8,3,2,48,1152]{4,3,2,1,0:T(8,128)(2,1)S(1)} %bitcast.34), channel_id=1, replica_groups=mesh['ma'=8,'row'=4] {'ma'}, dimensions={0} | all-to-all | bytes 10616832 | tf_op jit(solution)/shard_map/all_to_all | solution.py:315
  217.4 6.6 %all-to-all-start.4 = ((bf16[8,3,2,48,1152]{4,3,2,1,0:T(8,128)(2,1)}), bf16[8,3,2,48,1152]{4,3,2,1,0:T(8,128)(2,1)}, u32[]{:S(2)}, u32[]{:S(2)}) async-start(bf16[8,3,2,48,1152]{4,3,2,1,0:T(8,128)(2,1)} %get-tuple-element.12), calls=%async_computation.4 | async-start | bytes 10616832 | tf_op jit(solution)/shard_map/all_to_all | solution.py:315
  224.1 8.0 %cosine_convert_fusion = (bf16[1,8,48,1152]{3,2,0,1:T(8,128)(2,1)S(1)}, bf16[1,8,48,1152]{3,2,0,1:T(8,128)(2,1)S(1)}) fusion(s32[8,48]{1,0:T(8,128)S(1)} %mul.83), kind=kLoop, calls=%fused_computation.8 | loop fusion | flops 5308416 | bytes 1771008 | tf_op jit(solution)/shard_map/convert
  234.8 28.7 %shard_map.66 = bf16[8,3,2,48,1152]{4,3,2,1,0:T(8,128)(2,1)} custom-call(bf16[8,3,2,48,1152]{4,3,2,1,0:T(8,128)(2,1)} %all-to-all-done.move_ref, bf16[8,3,2,48,1152]{4,3,2,1,0:T(8,128)(2,1)} %all_to_all.30.spin_ref, bf16[1152,768]{1,0:T(8,128)(2,1)} %copy.7.across_ref, bf16[768,1152]{1,0:T(8,128)(2,1)} %bitcast.31), custom_call_target="tpu_custom_call" | custom-call | flops 18345885696 | bytes 15925248 | tf_op jit(solution)/shard_map/pallas_call | solution.py:129
  263.5 20.1 %all-to-all-done.4.spin_ref = bf16[8,3,2,48,1152]{4,3,2,1,0:T(8,128)(2,1)} async-done(((bf16[8,3,2,48,1152]{4,3,2,1,0:T(8,128)(2,1)}), bf16[8,3,2,48,1152]{4,3,2,1,0:T(8,128)(2,1)}, u32[]{:S(2)}, u32[]{:S(2)}) %all-to-all-start.4) | async-done | bytes 5308448 | tf_op jit(solution)/shard_map/all_to_all | solution.py:315
  283.6 6.4 %all-to-all-start.2 = ((bf16[8,3,2,48,1152]{4,3,2,1,0:T(8,128)(2,1)}), bf16[8,3,2,48,1152]{4,3,2,1,0:T(8,128)(2,1)}, u32[]{:S(2)}, u32[]{:S(2)}) async-start(bf16[8,3,2,48,1152]{4,3,2,1,0:T(8,128)(2,1)} %shard_map.66), calls=%async_computation.2 | async-start | bytes 10616832 | tf_op jit(solution)/shard_map/all_to_all | solution.py:315
  290.0 28.8 %shard_map.68 = bf16[8,3,2,48,1152]{4,3,2,1,0:T(8,128)(2,1)} custom-call(bf16[8,3,2,48,1152]{4,3,2,1,0:T(8,128)(2,1)} %all_to_all.31.move_ref, bf16[8,3,2,48,1152]{4,3,2,1,0:T(8,128)(2,1)} %all-to-all-done.4.spin_ref, bf16[1152,768]{1,0:T(8,128)(2,1)} %copy.7.across_ref, bf16[768,1152]{1,0:T(8,128)(2,1)} %bitcast.32), custom_call_target="tpu_custom_call" | custom-call | flops 18345885696 | bytes 15925248 | tf_op jit(solution)/shard_map/pallas_call | solution.py:129
  318.8 30.7 %all-to-all-done.2.in_ref = bf16[8,3,2,48,1152]{4,3,2,1,0:T(8,128)(2,1)} async-done(((bf16[8,3,2,48,1152]{4,3,2,1,0:T(8,128)(2,1)}), bf16[8,3,2,48,1152]{4,3,2,1,0:T(8,128)(2,1)}, u32[]{:S(2)}, u32[]{:S(2)}) %all-to-all-start.2) | async-done | bytes 5308448 | tf_op jit(solution)/shard_map/all_to_all | solution.py:315
  349.5 6.2 %all-to-all-start.5 = ((bf16[8,3,2,48,1152]{4,3,2,1,0:T(8,128)(2,1)}), bf16[8,3,2,48,1152]{4,3,2,1,0:T(8,128)(2,1)}, u32[]{:S(2)}, u32[]{:S(2)}) async-start(bf16[8,3,2,48,1152]{4,3,2,1,0:T(8,128)(2,1)} %shard_map.68), calls=%async_computation.5 | async-start | bytes 10616832 | tf_op jit(solution)/shard_map/all_to_all | solution.py:315
  355.7 15.4 %shard_map.67 = bf16[4,12,96,384]{3,2,1,0:T(8,128)(2,1)} custom-call(bf16[8,3,2,48,1152]{4,3,2,1,0:T(8,128)(2,1)} %all-to-all-done.2.in_ref, bf16[48,576,384]{2,1,0:T(8,128)(2,1)} %bitcast.26, bf16[3,2,48,32,384]{4,3,2,1,0:T(8,128)(2,1)} %velocity_ref.3), custom_call_target="tpu_custom_call" | custom-call | flops 2038431744 | bytes 42467328 | tf_op jit(solution)/shard_map/pallas_call | solution.py:194
  378.4 36.8 %all-to-all-done.5.in_ref = bf16[8,3,2,48,1152]{4,3,2,1,0:T(8,128)(2,1)} async-done(((bf16[8,3,2,48,1152]{4,3,2,1,0:T(8,128)(2,1)}), bf16[8,3,2,48,1152]{4,3,2,1,0:T(8,128)(2,1)}, u32[]{:S(2)}, u32[]{:S(2)}) %all-to-all-start.5) | async-done | bytes 5308448 | tf_op jit(solution)/shard_map/all_to_all | solution.py:315
  415.3 15.5 %shard_map.69 = bf16[4,12,96,384]{3,2,1,0:T(8,128)(2,1)} custom-call(bf16[8,3,2,48,1152]{4,3,2,1,0:T(8,128)(2,1)} %all-to-all-done.5.in_ref, bf16[48,576,384]{2,1,0:T(8,128)(2,1)} %bitcast.27, bf16[3,2,48,32,384]{4,3,2,1,0:T(8,128)(2,1)} %velocity_ref.3), custom_call_target="tpu_custom_call" | custom-call | flops 2038431744 | bytes 42467328 | tf_op jit(solution)/shard_map/pallas_call | solution.py:194
  430.7 3.6 dynamic-slice_bitcast_fusion
  438.1 5.4 copy.9
  445.3 6.0 %collective-permute-done.1.refs_2_ = bf16[12,96,384]{2,1,0:T(8,128)(2,1)} collective-permute-done((bf16[12,96,384]{2,1,0:T(8,128)(2,1)S(1)}, bf16[12,96,384]{2,1,0:T(8,128)(2,1)}, u32[]{:S(2)}, u32[]{:S(2)}) %collective-permute-start.1) | collective-permute-done | bytes 884768 | tf_op jit(solution)/shard_map/ppermute | solution.py:288
  451.3 40.5 %collective-permute-done.2.refs_3_ = bf16[12,96,384]{2,1,0:T(8,128)(2,1)} collective-permute-done((bf16[12,96,384]{2,1,0:T(8,128)(2,1)S(1)}, bf16[12,96,384]{2,1,0:T(8,128)(2,1)}, u32[]{:S(2)}, u32[]{:S(2)}) %collective-permute-start.2) | collective-permute-done | bytes 884768 | tf_op jit(solution)/shard_map/ppermute | solution.py:288
  491.8 16.5 %collective-permute-done.3.refs_5_ = bf16[12,96,384]{2,1,0:T(8,128)(2,1)} collective-permute-done((bf16[12,96,384]{2,1,0:T(8,128)(2,1)}, bf16[12,96,384]{2,1,0:T(8,128)(2,1)}, u32[]{:S(2)}, u32[]{:S(2)}) %collective-permute-start.3) | collective-permute-done | bytes 884768 | tf_op jit(solution)/shard_map/ppermute | solution.py:288
  508.3 19.0 %collective-permute-done.4.refs_6_ = bf16[12,96,384]{2,1,0:T(8,128)(2,1)} collective-permute-done((bf16[12,96,384]{2,1,0:T(8,128)(2,1)}, bf16[12,96,384]{2,1,0:T(8,128)(2,1)}, u32[]{:S(2)}, u32[]{:S(2)}) %collective-permute-start.4) | collective-permute-done | bytes 884768 | tf_op jit(solution)/shard_map/ppermute | solution.py:288
  530.6 31.9 %shard_map.70 = f32[3,2,48,96,128]{4,3,2,1,0:T(8,128)} custom-call(bf16[12,96,384]{2,1,0:T(8,128)(2,1)} %get-tuple-element.20.refs_0_, bf16[12,96,384]{2,1,0:T(8,128)(2,1)} %collective-permute-done.refs_1_, bf16[12,96,384]{2,1,0:T(8,128)(2,1)} %collective-permute-done.1.refs_2_, bf16[12,96,384]{2,1,0:T(8,128)(2,1)} %collective-permute-done.2.refs_3_, ...), custom_call_target="tpu_custom_call" | custom-call | flops 7247757312 | bytes 21233664 | tf_op jit(solution)/shard_map/pallas_call | solution.py:261
  (26 shorter events, 20.3 us)
Async XLA Ops:
  22.3 65.0 %all-to-all-start = ((bf16[8,3,2,48,1152]{4,3,2,1,0:T(8,128)(2,1)}), bf16[8,3,2,48,1152]{4,3,2,1,0:T(8,128)(2,1)}, u32[]{:S(2)}, u32[]{:S(2)}) async-start(bf16[8,3,2,48,1152]{4,3,2,1,0:T(8,128)(2,1)} %get-tuple-element.9), calls=%async_computation | async-start | bytes 10616832 | tf_op jit(solution)/shard_map/all_to_all | solution.py:315
  87.3 65.9 %slice-start = ((s8[5308416]{0:T(1024)(128)(4,1)}), s8[4194304]{0:T(1024)(128)(4,1)S(1)}, s32[]{:S(2)}) async-start(s8[5308416]{0:T(1024)(128)(4,1)} %bitcast.33), calls=%async_computation.6 | async-start | bytes 8388608
  87.3 65.9 %slice-start.1 = ((s8[5308416]{0:T(1024)(128)(4,1)}), s8[1114112]{0:T(1024)(128)(4,1)S(1)}, s32[]{:S(2)}) async-start(s8[5308416]{0:T(1024)(128)(4,1)} %bitcast.33), calls=%async_computation.7 | async-start | bytes 2228224
  217.4 6.6 %copy-start.1 = (s32[384]{0:T(512)S(1)}, s32[384]{0:T(512)}, u32[]{:S(2)}) copy-start(s32[384]{0:T(512)} %param.8) | copy-start | bytes 4612
  217.4 66.1 %all-to-all-start.4 = ((bf16[8,3,2,48,1152]{4,3,2,1,0:T(8,128)(2,1)}), bf16[8,3,2,48,1152]{4,3,2,1,0:T(8,128)(2,1)}, u32[]{:S(2)}, u32[]{:S(2)}) async-start(bf16[8,3,2,48,1152]{4,3,2,1,0:T(8,128)(2,1)} %get-tuple-element.12), calls=%async_computation.4 | async-start | bytes 10616832 | tf_op jit(solution)/shard_map/all_to_all | solution.py:315
  232.3 2.5 copy-start
  283.6 65.9 %all-to-all-start.2 = ((bf16[8,3,2,48,1152]{4,3,2,1,0:T(8,128)(2,1)}), bf16[8,3,2,48,1152]{4,3,2,1,0:T(8,128)(2,1)}, u32[]{:S(2)}, u32[]{:S(2)}) async-start(bf16[8,3,2,48,1152]{4,3,2,1,0:T(8,128)(2,1)} %shard_map.66), calls=%async_computation.2 | async-start | bytes 10616832 | tf_op jit(solution)/shard_map/all_to_all | solution.py:315
  349.5 65.7 %all-to-all-start.5 = ((bf16[8,3,2,48,1152]{4,3,2,1,0:T(8,128)(2,1)}), bf16[8,3,2,48,1152]{4,3,2,1,0:T(8,128)(2,1)}, u32[]{:S(2)}, u32[]{:S(2)}) async-start(bf16[8,3,2,48,1152]{4,3,2,1,0:T(8,128)(2,1)} %shard_map.68), calls=%async_computation.5 | async-start | bytes 10616832 | tf_op jit(solution)/shard_map/all_to_all | solution.py:315
  374.4 62.2 %collective-permute-start = (bf16[12,96,384]{2,1,0:T(8,128)(2,1)S(1)}, bf16[12,96,384]{2,1,0:T(8,128)(2,1)}, u32[]{:S(2)}, u32[]{:S(2)}) collective-permute-start(bf16[12,96,384]{2,1,0:T(8,128)(2,1)S(1)} %get-tuple-element.19), channel_id=1, source_target_pairs={{0,1},{1,2},{2,3},{3,0},{4,5},{5,6},{6,7},{7,4},{8,9},{9,10},{10,1... | collective-permute-start | bytes 2654216 | tf_op jit(solution)/shard_map/ppermute | solution.py:288
  375.7 75.6 %collective-permute-start.1 = (bf16[12,96,384]{2,1,0:T(8,128)(2,1)S(1)}, bf16[12,96,384]{2,1,0:T(8,128)(2,1)}, u32[]{:S(2)}, u32[]{:S(2)}) collective-permute-start(bf16[12,96,384]{2,1,0:T(8,128)(2,1)S(1)} %get-tuple-element.18), channel_id=1, source_target_pairs={{0,2},{1,3},{2,0},{3,1},{4,6},{5,7},{6,4},{7,5},{8,10},{9,11},{10,... | collective-permute-start | bytes 2654216 | tf_op jit(solution)/shard_map/ppermute | solution.py:288
  376.7 115.0 %collective-permute-start.2 = (bf16[12,96,384]{2,1,0:T(8,128)(2,1)S(1)}, bf16[12,96,384]{2,1,0:T(8,128)(2,1)}, u32[]{:S(2)}, u32[]{:S(2)}) collective-permute-start(bf16[12,96,384]{2,1,0:T(8,128)(2,1)S(1)} %get-tuple-element.17), channel_id=1, source_target_pairs={{0,3},{1,0},{2,1},{3,2},{4,7},{5,4},{6,5},{7,6},{8,11},{9,8},{10,9... | collective-permute-start | bytes 2654216 | tf_op jit(solution)/shard_map/ppermute | solution.py:288
  434.4 73.9 %collective-permute-start.3 = (bf16[12,96,384]{2,1,0:T(8,128)(2,1)}, bf16[12,96,384]{2,1,0:T(8,128)(2,1)}, u32[]{:S(2)}, u32[]{:S(2)}) collective-permute-start(bf16[12,96,384]{2,1,0:T(8,128)(2,1)} %get-tuple-element.15), channel_id=1, source_target_pairs={{0,1},{1,2},{2,3},{3,0},{4,5},{5,6},{6,7},{7,4},{8,9},{9,10},{10,1... | collective-permute-start | bytes 2654216 | tf_op jit(solution)/shard_map/ppermute | solution.py:288
  435.7 91.6 %collective-permute-start.4 = (bf16[12,96,384]{2,1,0:T(8,128)(2,1)}, bf16[12,96,384]{2,1,0:T(8,128)(2,1)}, u32[]{:S(2)}, u32[]{:S(2)}) collective-permute-start(bf16[12,96,384]{2,1,0:T(8,128)(2,1)} %get-tuple-element.14), channel_id=1, source_target_pairs={{0,2},{1,3},{2,0},{3,1},{4,6},{5,7},{6,4},{7,5},{8,10},{9,11},{10,... | collective-permute-start | bytes 2654216 | tf_op jit(solution)/shard_map/ppermute | solution.py:288
  436.7 92.9 %collective-permute-start.5 = (bf16[12,96,384]{2,1,0:T(8,128)(2,1)S(1)}, bf16[12,96,384]{2,1,0:T(8,128)(2,1)S(1)}, u32[]{:S(2)}, u32[]{:S(2)}) collective-permute-start(bf16[12,96,384]{2,1,0:T(8,128)(2,1)S(1)} %get-tuple-element.13), channel_id=1, source_target_pairs={{0,3},{1,0},{2,1},{3,2},{4,7},{5,4},{6,5},{7,6},{8,11},{9,8},{10,9... | collective-permute-start | bytes 2654216 | tf_op jit(solution)/shard_map/ppermute | solution.py:288
  529.6 0.9 copy-start.2

commit v4 on v3

--- a/solution.py
+++ b/solution.py
@@ -211,7 +211,8 @@
     )(back, table, velocity)
 
 
-def radial_kernel(*refs):
+def radial_kernel(begun, *refs):
+    refs = refs[1:] if begun else refs
     *piece_refs, order_ref, operator_ref, out_ref, lines, solved = refs
     quads, own, wide = piece_refs[0].shape
     comps, parts, slots = out_ref.shape[:3]
@@ -253,29 +254,34 @@
     return (target[:, None] == columns[None, :]).astype(jnp.bfloat16)
 
 
-def radial_solve(pieces, order, operators, comps, parts, slots):
+def radial_solve(pieces, order, operators, comps, parts, slots, part, done):
     quads, own, wide = pieces[0].shape
+    begun = [] if done is None else [done]
     full = operators.shape[1]
     block = pl.BlockSpec((quads, 2 * ROWS, wide), lambda i: (0, i, 0))
-    scratch = pltpu.VMEM((comps * parts * slots * 2 * ROWS, LANES), jnp.float32)
+    scratch = pltpu.VMEM((comps * parts * quads * QUAD * 2 * ROWS, LANES), jnp.float32)
     return pl.pallas_call(
-        radial_kernel,
+        functools.partial(radial_kernel, bool(begun)),
         grid=(own // (2 * ROWS),),
-        in_specs=[block] * len(pieces)
+        in_specs=[pl.BlockSpec(memory_space=pl.ANY)] * len(begun)
+        + [block] * len(pieces)
         + [
             pl.BlockSpec(order.shape, lambda i: (0, 0)),
             pl.BlockSpec((2 * ROWS, full, full), lambda i: (i, 0, 0)),
         ],
-        out_specs=pl.BlockSpec((comps, parts, slots, 2 * ROWS, full), lambda i: (0, 0, 0, i, 0)),
+        out_specs=pl.BlockSpec(
+            (comps, parts, quads * QUAD, 2 * ROWS, full), lambda i: (0, 0, part, i, 0)
+        ),
         out_shape=jax.ShapeDtypeStruct((comps, parts, slots, own, full), jnp.float32),
         scratch_shapes=[scratch, scratch],
+        input_output_aliases={0: 0} if begun else {},
         compiler_params=pltpu.CompilerParams(vmem_limit_bytes=56 << 20),
         cost_estimate=pl.CostEstimate(
             flops=2 * len(pieces) * pieces[0].size * order.shape[0],
             bytes_accessed=6 * len(pieces) * pieces[0].size,
             transcendentals=0,
         ),
-    )(*pieces, order, operators)
+    )(*begun, *pieces, order, operators)
 
 
 def share_degrees(sides, groups):
@@ -326,12 +332,24 @@
     early = exchange(through_grid(move_early, spin_early, across, along, NL / NLON))
     late = exchange(through_grid(move_late, spin_late, across, along, NL / NLON))
     groups = lax.axis_size("row")
-    pieces = []
-    for h, back in enumerate((early, late)):
-        pieces += share_degrees(analyze(h, back, weights, velocity, groups), groups)
+    halves = [
+        analyze(h, back, weights, velocity, groups) for h, back in enumerate((early, late))
+    ]
+    quads = ROWS // QUAD
+    thirds = [
+        [
+            piece
+            for sides in halves
+            for piece in share_degrees(sides[:, i : i + quads], groups)
+        ]
+        for i in range(0, slots // QUAD, quads)
+    ]
     order = radial_order(groups, owners, groups * velocity.shape[3], lax.axis_index("row"))
     operators = jnp.transpose(inverse_operators, (0, 2, 1)).astype(jnp.bfloat16)
-    return radial_solve(pieces, order, operators, *velocity.shape[:3])
+    done = None
+    for part, pieces in enumerate(thirds):
+        done = radial_solve(pieces, order, operators, *velocity.shape[:3], part, done)
+    return done
 
 
 def per_device(velocity, vorticity, order_table, legendre_bf, weighted, inverse_operators):

time: 569 us -> 592 us (1.040)
  the two profiles are of different devices: /device:TPU:11 before, /device:TPU:0 now
where the time goes in v4:
time: 592 us; the launch traced here: 586 us
  waiting for transfers between devices  188 us (32%)
  Pallas kernels  170 us (29%)
  blocking collectives  132 us (22%)
  starting transfers between devices  63.6 us (11%)
  local copies, waits for them, and re-layouts  20.2 us (3%)
  other arithmetic  11.2 us (2%)
    all_to_all x2, blocking collectives, exchange(): return lax.all_to_all(x, 'ma', split_axis=0, concat_axis=0, tiled=True)  132 us
    all_to_all x4, waiting for transfers between devices, exchange(): return lax.all_to_all(x, 'ma', split_axis=0, concat_axis=0, tiled=True)  130 us
    ppermute x18, waiting for transfers between devices, share_degrees(): block = lax.ppermute(block, 'row', places)  58.7 us
    pallas_call x2, Pallas kernels, through_grid(): pl.pallas_call(functools.partial(grid_kernel, scale), grid=(columns // wi...  57.5 us
    ppermute x18, starting transfers between devices, share_degrees(): block = lax.ppermute(block, 'row', places)  44.2 us
    pallas_call x2, Pallas kernels, synthesize(): pl.pallas_call(synth_kernel, grid=(slots // ROWS,), in_specs=[pl.BlockSpe...  42 us
    pallas_call x3, Pallas kernels, radial_solve(): pl.pallas_call(functools.partial(radial_kernel, bool(begun)), grid=(own /...  39.1 us
    pallas_call x2, Pallas kernels, analyze(): pl.pallas_call(functools.partial(analyze_kernel, h), grid=(slots // ROWS,...  31 us
  transfers between devices with their start and end apart: 22, of which 7 were waited for; matrix products, arithmetic and copies ran while one was open for 5% of the time, Pallas kernels for 23%

profile of v4, /device:TPU:0, one launch (start us, length us, event | category | flops | bytes accessed | tf_op | source)
XLA Modules:
  0.0 585.6 jit_solution(7495894148888703329)
XLA Ops:
  1.3 21.0 %shard_map.65 = (bf16[8,3,2,48,1152]{4,3,2,1,0:T(8,128)(2,1)}, bf16[8,3,2,48,1152]{4,3,2,1,0:T(8,128)(2,1)}) custom-call(f32[48]{0:T(128)} %fusion.31.scale_ref, bf16[3,2,48,32,384]{4,3,2,1,0:T(8,128)(2,1)} %spec_ref.3, bf16[48,576,384]{2,1,0:T(8,128)(2,1)} %bitcast.60), custom_call_target="tpu_custom_call" | custom-call | flops 4076863488 | bytes 38928384 | tf_op jit(solution)/shard_map/pallas_call | solution.py:77
  22.2 66.3 %all_to_all.30.spin_ref = bf16[8,3,2,48,1152]{4,3,2,1,0:T(8,128)(2,1)} all-to-all(bf16[8,3,2,48,1152]{4,3,2,1,0:T(8,128)(2,1)} %get-tuple-element.10), channel_id=1, replica_groups=mesh['ma'=8,'row'=4] {'ma'}, dimensions={0} | all-to-all | bytes 10616832 | tf_op jit(solution)/shard_map/all_to_all | solution.py:321
  93.2 21.0 %shard_map.64 = (bf16[8,3,2,48,1152]{4,3,2,1,0:T(8,128)(2,1)}, bf16[8,3,2,48,1152]{4,3,2,1,0:T(8,128)(2,1)}) custom-call(f32[48]{0:T(128)} %fusion.31.scale_ref, bf16[3,2,48,32,384]{4,3,2,1,0:T(8,128)(2,1)} %velocity_ref.3, bf16[48,576,384]{2,1,0:T(8,128)(2,1)} %bitcast.61), custom_call_target="tpu_custom_call" | custom-call | flops 4076863488 | bytes 38928384 | tf_op jit(solution)/shard_map/pallas_call | solution.py:77
  114.2 40.1 %all-to-all-done.4.spin_ref = bf16[8,3,2,48,1152]{4,3,2,1,0:T(8,128)(2,1)} async-done(((bf16[8,3,2,48,1152]{4,3,2,1,0:T(8,128)(2,1)}), bf16[8,3,2,48,1152]{4,3,2,1,0:T(8,128)(2,1)}, u32[]{:S(2)}, u32[]{:S(2)}) %all-to-all-start.4) | async-done | bytes 5308448 | tf_op jit(solution)/shard_map/all_to_all | solution.py:321
  154.2 65.5 %all_to_all.31.move_ref = bf16[8,3,2,48,1152]{4,3,2,1,0:T(8,128)(2,1)} all-to-all(bf16[8,3,2,48,1152]{4,3,2,1,0:T(8,128)(2,1)} %get-tuple-element.11), channel_id=1, replica_groups=mesh['ma'=8,'row'=4] {'ma'}, dimensions={0} | all-to-all | bytes 10616832 | tf_op jit(solution)/shard_map/all_to_all | solution.py:321
  219.8 5.3 all-to-all-start
  225.2 8.0 %cosine_convert_fusion = (bf16[1,8,48,1152]{3,2,0,1:T(8,128)(2,1)S(1)}, bf16[1,8,48,1152]{3,2,0,1:T(8,128)(2,1)S(1)}) fusion(s32[8,48]{1,0:T(8,128)S(1)} %mul.83), kind=kLoop, calls=%fused_computation.8 | loop fusion | flops 5308416 | bytes 1771008 | tf_op jit(solution)/shard_map/convert
  235.8 28.8 %shard_map.68 = bf16[8,3,2,48,1152]{4,3,2,1,0:T(8,128)(2,1)} custom-call(bf16[8,3,2,48,1152]{4,3,2,1,0:T(8,128)(2,1)} %all_to_all.31.move_ref, bf16[8,3,2,48,1152]{4,3,2,1,0:T(8,128)(2,1)} %all-to-all-done.4.spin_ref, bf16[1152,768]{1,0:T(8,128)(2,1)} %copy.9.across_ref, bf16[768,1152]{1,0:T(8,128)(2,1)} %bitcast.66), custom_call_target="tpu_custom_call" | custom-call | flops 18345885696 | bytes 15925248 | tf_op jit(solution)/shard_map/pallas_call | solution.py:129
  264.6 21.5 %all-to-all-done.move_ref = bf16[8,3,2,48,1152]{4,3,2,1,0:T(8,128)(2,1)} async-done(((bf16[8,3,2,48,1152]{4,3,2,1,0:T(8,128)(2,1)}), bf16[8,3,2,48,1152]{4,3,2,1,0:T(8,128)(2,1)}, u32[]{:S(2)}, u32[]{:S(2)}) %all-to-all-start) | async-done | bytes 5308448 | tf_op jit(solution)/shard_map/all_to_all | solution.py:321
  286.2 4.8 all-to-all-start.5
  291.0 28.7 %shard_map.66 = bf16[8,3,2,48,1152]{4,3,2,1,0:T(8,128)(2,1)} custom-call(bf16[8,3,2,48,1152]{4,3,2,1,0:T(8,128)(2,1)} %all-to-all-done.move_ref, bf16[8,3,2,48,1152]{4,3,2,1,0:T(8,128)(2,1)} %all_to_all.30.spin_ref, bf16[1152,768]{1,0:T(8,128)(2,1)} %copy.9.across_ref, bf16[768,1152]{1,0:T(8,128)(2,1)} %bitcast.67), custom_call_target="tpu_custom_call" | custom-call | flops 18345885696 | bytes 15925248 | tf_op jit(solution)/shard_map/pallas_call | solution.py:129
  319.8 32.3 %all-to-all-done.5.in_ref = bf16[8,3,2,48,1152]{4,3,2,1,0:T(8,128)(2,1)} async-done(((bf16[8,3,2,48,1152]{4,3,2,1,0:T(8,128)(2,1)}), bf16[8,3,2,48,1152]{4,3,2,1,0:T(8,128)(2,1)}, u32[]{:S(2)}, u32[]{:S(2)}) %all-to-all-start.5) | async-done | bytes 5308448 | tf_op jit(solution)/shard_map/all_to_all | solution.py:321
  356.8 15.5 %shard_map.69 = bf16[4,12,96,384]{3,2,1,0:T(8,128)(2,1)} custom-call(bf16[8,3,2,48,1152]{4,3,2,1,0:T(8,128)(2,1)} %all-to-all-done.5.in_ref, bf16[48,576,384]{2,1,0:T(8,128)(2,1)} %bitcast.58, bf16[3,2,48,32,384]{4,3,2,1,0:T(8,128)(2,1)} %velocity_ref.3), custom_call_target="tpu_custom_call" | custom-call | flops 2038431744 | bytes 42467328 | tf_op jit(solution)/shard_map/pallas_call | solution.py:194
  382.0 35.8 %all-to-all-done.2.in_ref = bf16[8,3,2,48,1152]{4,3,2,1,0:T(8,128)(2,1)} async-done(((bf16[8,3,2,48,1152]{4,3,2,1,0:T(8,128)(2,1)}), bf16[8,3,2,48,1152]{4,3,2,1,0:T(8,128)(2,1)}, u32[]{:S(2)}, u32[]{:S(2)}) %all-to-all-start.2) | async-done | bytes 5308448 | tf_op jit(solution)/shard_map/all_to_all | solution.py:321
  417.8 15.4 %shard_map.67 = bf16[4,12,96,384]{3,2,1,0:T(8,128)(2,1)} custom-call(bf16[8,3,2,48,1152]{4,3,2,1,0:T(8,128)(2,1)} %all-to-all-done.2.in_ref, bf16[48,576,384]{2,1,0:T(8,128)(2,1)} %bitcast.59, bf16[3,2,48,32,384]{4,3,2,1,0:T(8,128)(2,1)} %velocity_ref.3), custom_call_target="tpu_custom_call" | custom-call | flops 2038431744 | bytes 42467328 | tf_op jit(solution)/shard_map/pallas_call | solution.py:194
  446.9 5.4 copy.11
  453.1 8.9 %collective-permute-start.7 = (bf16[4,96,384]{2,1,0:T(8,128)(2,1)S(1)}, bf16[4,96,384]{2,1,0:T(8,128)(2,1)S(1)}, u32[]{:S(2)}, u32[]{:S(2)}) collective-permute-start(bf16[4,96,384]{2,1,0:T(8,128)(2,1)S(1)} %get-tuple-element.32), channel_id=1, source_target_pairs={{0,2},{1,3},{2,0},{3,1},{4,6},{5,7},{6,4},{7,5},{8,10},{9,11},{10,... | collective-permute-start | bytes 884744 | tf_op jit(solution)/shard_map/ppermute | solution.py:294
  463.6 18.5 %collective-permute-done.4.refs_6_ = bf16[4,96,384]{2,1,0:T(8,128)(2,1)} collective-permute-done((bf16[4,96,384]{2,1,0:T(8,128)(2,1)}, bf16[4,96,384]{2,1,0:T(8,128)(2,1)}, u32[]{:S(2)}, u32[]{:S(2)}) %collective-permute-start.4) | collective-permute-done | bytes 294944 | tf_op jit(solution)/shard_map/ppermute | solution.py:294
  482.1 13.6 %collective-permute-start.1 = (bf16[4,96,384]{2,1,0:T(8,128)(2,1)S(1)}, bf16[4,96,384]{2,1,0:T(8,128)(2,1)S(1)}, u32[]{:S(2)}, u32[]{:S(2)}) collective-permute-start(bf16[4,96,384]{2,1,0:T(8,128)(2,1)S(1)} %get-tuple-element.40), channel_id=1, source_target_pairs={{0,2},{1,3},{2,0},{3,1},{4,6},{5,7},{6,4},{7,5},{8,10},{9,11},{10,... | collective-permute-start | bytes 884744 | tf_op jit(solution)/shard_map/ppermute | solution.py:294
  500.1 15.6 %collective-permute-done.7.refs_3_ = bf16[4,96,384]{2,1,0:T(8,128)(2,1)S(1)} collective-permute-done((bf16[4,96,384]{2,1,0:T(8,128)(2,1)S(1)}, bf16[4,96,384]{2,1,0:T(8,128)(2,1)S(1)}, u32[]{:S(2)}, u32[]{:S(2)}) %collective-permute-start.7) | collective-permute-done | bytes 294944 | tf_op jit(solution)/shard_map/ppermute | solution.py:294
  519.6 24.6 %collective-permute-done.1.refs_2_ = bf16[4,96,384]{2,1,0:T(8,128)(2,1)S(1)} collective-permute-done((bf16[4,96,384]{2,1,0:T(8,128)(2,1)S(1)}, bf16[4,96,384]{2,1,0:T(8,128)(2,1)S(1)}, u32[]{:S(2)}, u32[]{:S(2)}) %collective-permute-start.1) | collective-permute-done | bytes 294944 | tf_op jit(solution)/shard_map/ppermute | solution.py:294
  545.0 13.0 %shard_map.70.refs_0_ = f32[3,2,48,96,128]{4,3,2,1,0:T(8,128)} custom-call(bf16[4,96,384]{2,1,0:T(8,128)(2,1)} %get-tuple-element.42.refs_0_, bf16[4,96,384]{2,1,0:T(8,128)(2,1)} %copy-done.6, bf16[4,96,384]{2,1,0:T(8,128)(2,1)} %copy-done.5, bf16[4,96,384]{2,1,0:T(8,128)(2,1)} %copy-done.4, bf16[4,96,384]{2,1,0:T(8,128)(2,1)} %get-tuple-element.38.refs_4_, ...), custom_call_target="tpu_custom_call" | custom-call | flops 2415919104 | bytes 7077888 | tf_op jit(solution)/shard_map/pallas_call | solution.py:263
  558.1 13.0 %shard_map.71.refs_0_ = f32[3,2,48,96,128]{4,3,2,1,0:T(8,128)} custom-call(f32[3,2,48,96,128]{4,3,2,1,0:T(8,128)} %shard_map.70.refs_0_, bf16[4,96,384]{2,1,0:T(8,128)(2,1)} %get-tuple-element.34.refs_1_, bf16[4,96,384]{2,1,0:T(8,128)(2,1)} %copy-done.8, bf16[4,96,384]{2,1,0:T(8,128)(2,1)} %copy-done.7, ...), custom_call_target="tpu_custom_call", output_to_operand_aliasing={{}: (0, {})} | custom-call | flops 2415919104 | bytes 7077888 | tf_op jit(solution)/shard_map/pallas_call | solution.py:263
  572.3 13.0 %shard_map.72 = f32[3,2,48,96,128]{4,3,2,1,0:T(8,128)} custom-call(f32[3,2,48,96,128]{4,3,2,1,0:T(8,128)} %shard_map.71.refs_0_, bf16[4,96,384]{2,1,0:T(8,128)(2,1)} %get-tuple-element.26.refs_1_, bf16[4,96,384]{2,1,0:T(8,128)(2,1)} %copy-done.13, bf16[4,96,384]{2,1,0:T(8,128)(2,1)} %copy-done.12, ...), custom_call_target="tpu_custom_call", output_to_operand_aliasing={{}: (0, {})} | custom-call | flops 2415919104 | bytes 7077888 | tf_op jit(solution)/shard_map/pallas_call | solution.py:263
  (77 shorter events, 49.2 us)
Async XLA Ops:
  88.5 65.7 %all-to-all-start.4 = ((bf16[8,3,2,48,1152]{4,3,2,1,0:T(8,128)(2,1)}), bf16[8,3,2,48,1152]{4,3,2,1,0:T(8,128)(2,1)}, u32[]{:S(2)}, u32[]{:S(2)}) async-start(bf16[8,3,2,48,1152]{4,3,2,1,0:T(8,128)(2,1)} %get-tuple-element.12), calls=%async_computation.4 | async-start | bytes 10616832 | tf_op jit(solution)/shard_map/all_to_all | solution.py:321
  219.8 66.4 %all-to-all-start = ((bf16[8,3,2,48,1152]{4,3,2,1,0:T(8,128)(2,1)}), bf16[8,3,2,48,1152]{4,3,2,1,0:T(8,128)(2,1)}, u32[]{:S(2)}, u32[]{:S(2)}) async-start(bf16[8,3,2,48,1152]{4,3,2,1,0:T(8,128)(2,1)} %get-tuple-element.9), calls=%async_computation | async-start | bytes 10616832 | tf_op jit(solution)/shard_map/all_to_all | solution.py:321
  286.2 65.9 %all-to-all-start.5 = ((bf16[8,3,2,48,1152]{4,3,2,1,0:T(8,128)(2,1)}), bf16[8,3,2,48,1152]{4,3,2,1,0:T(8,128)(2,1)}, u32[]{:S(2)}, u32[]{:S(2)}) async-start(bf16[8,3,2,48,1152]{4,3,2,1,0:T(8,128)(2,1)} %shard_map.68), calls=%async_computation.5 | async-start | bytes 10616832 | tf_op jit(solution)/shard_map/all_to_all | solution.py:321
  352.1 65.8 %all-to-all-start.2 = ((bf16[8,3,2,48,1152]{4,3,2,1,0:T(8,128)(2,1)}), bf16[8,3,2,48,1152]{4,3,2,1,0:T(8,128)(2,1)}, u32[]{:S(2)}, u32[]{:S(2)}) async-start(bf16[8,3,2,48,1152]{4,3,2,1,0:T(8,128)(2,1)} %shard_map.66), calls=%async_computation.2 | async-start | bytes 10616832 | tf_op jit(solution)/shard_map/all_to_all | solution.py:321
  376.0 66.1 %collective-permute-start.17 = (bf16[4,96,384]{2,1,0:T(8,128)(2,1)}, bf16[4,96,384]{2,1,0:T(8,128)(2,1)}, u32[]{:S(2)}, u32[]{:S(2)}) collective-permute-start(bf16[4,96,384]{2,1,0:T(8,128)(2,1)} %get-tuple-element.19), channel_id=1, source_target_pairs={{0,3},{1,0},{2,1},{3,2},{4,7},{5,4},{6,5},{7,6},{8,11},{9,8},{10,9... | collective-permute-start | bytes 884744 | tf_op jit(solution)/shard_map/ppermute | solution.py:294
  381.4 61.7 %collective-permute-start.11 = (bf16[4,96,384]{2,1,0:T(8,128)(2,1)}, bf16[4,96,384]{2,1,0:T(8,128)(2,1)}, u32[]{:S(2)}, u32[]{:S(2)}) collective-permute-start(bf16[4,96,384]{2,1,0:T(8,128)(2,1)} %get-tuple-element.27), channel_id=1, source_target_pairs={{0,3},{1,0},{2,1},{3,2},{4,7},{5,4},{6,5},{7,6},{8,11},{9,8},{10,9... | collective-permute-start | bytes 884744 | tf_op jit(solution)/shard_map/ppermute | solution.py:294
  382.0 62.6 %collective-permute-start.10 = (bf16[4,96,384]{2,1,0:T(8,128)(2,1)}, bf16[4,96,384]{2,1,0:T(8,128)(2,1)}, u32[]{:S(2)}, u32[]{:S(2)}) collective-permute-start(bf16[4,96,384]{2,1,0:T(8,128)(2,1)} %get-tuple-element.28), channel_id=1, source_target_pairs={{0,2},{1,3},{2,0},{3,1},{4,6},{5,7},{6,4},{7,5},{8,10},{9,11},{10,... | collective-permute-start | bytes 884744 | tf_op jit(solution)/shard_map/ppermute | solution.py:294
  435.8 17.4 %collective-permute-start.9 = (bf16[4,96,384]{2,1,0:T(8,128)(2,1)}, bf16[4,96,384]{2,1,0:T(8,128)(2,1)}, u32[]{:S(2)}, u32[]{:S(2)}) collective-permute-start(bf16[4,96,384]{2,1,0:T(8,128)(2,1)} %get-tuple-element.29), channel_id=1, source_target_pairs={{0,1},{1,2},{2,3},{3,0},{4,5},{5,6},{6,7},{7,4},{8,9},{9,10},{10,1... | collective-permute-start | bytes 884744 | tf_op jit(solution)/shard_map/ppermute | solution.py:294
  439.2 22.8 %collective-permute-start.5 = (bf16[4,96,384]{2,1,0:T(8,128)(2,1)}, bf16[4,96,384]{2,1,0:T(8,128)(2,1)S(1)}, u32[]{:S(2)}, u32[]{:S(2)}) collective-permute-start(bf16[4,96,384]{2,1,0:T(8,128)(2,1)} %get-tuple-element.35), channel_id=1, source_target_pairs={{0,3},{1,0},{2,1},{3,2},{4,7},{5,4},{6,5},{7,6},{8,11},{9,8},{10,9... | collective-permute-start | bytes 884744 | tf_op jit(solution)/shard_map/ppermute | solution.py:294
  442.1 40.0 %collective-permute-start.4 = (bf16[4,96,384]{2,1,0:T(8,128)(2,1)}, bf16[4,96,384]{2,1,0:T(8,128)(2,1)}, u32[]{:S(2)}, u32[]{:S(2)}) collective-permute-start(bf16[4,96,384]{2,1,0:T(8,128)(2,1)} %get-tuple-element.36), channel_id=1, source_target_pairs={{0,2},{1,3},{2,0},{3,1},{4,6},{5,7},{6,4},{7,5},{8,10},{9,11},{10,... | collective-permute-start | bytes 884744 | tf_op jit(solution)/shard_map/ppermute | solution.py:294
  443.1 39.0 %collective-permute-start.3 = (bf16[4,96,384]{2,1,0:T(8,128)(2,1)}, bf16[4,96,384]{2,1,0:T(8,128)(2,1)}, u32[]{:S(2)}, u32[]{:S(2)}) collective-permute-start(bf16[4,96,384]{2,1,0:T(8,128)(2,1)} %get-tuple-element.37), channel_id=1, source_target_pairs={{0,1},{1,2},{2,3},{3,0},{4,5},{5,6},{6,7},{7,4},{8,9},{9,10},{10,1... | collective-permute-start | bytes 884744 | tf_op jit(solution)/shard_map/ppermute | solution.py:294
  444.7 51.1 %collective-permute-start.8 = (bf16[4,96,384]{2,1,0:T(8,128)(2,1)S(1)}, bf16[4,96,384]{2,1,0:T(8,128)(2,1)}, u32[]{:S(2)}, u32[]{:S(2)}) collective-permute-start(bf16[4,96,384]{2,1,0:T(8,128)(2,1)S(1)} %get-tuple-element.31), channel_id=1, source_target_pairs={{0,3},{1,0},{2,1},{3,2},{4,7},{5,4},{6,5},{7,6},{8,11},{9,8},{10,9... | collective-permute-start | bytes 884744 | tf_op jit(solution)/shard_map/ppermute | solution.py:294
  453.1 62.6 %collective-permute-start.7 = (bf16[4,96,384]{2,1,0:T(8,128)(2,1)S(1)}, bf16[4,96,384]{2,1,0:T(8,128)(2,1)S(1)}, u32[]{:S(2)}, u32[]{:S(2)}) collective-permute-start(bf16[4,96,384]{2,1,0:T(8,128)(2,1)S(1)} %get-tuple-element.32), channel_id=1, source_target_pairs={{0,2},{1,3},{2,0},{3,1},{4,6},{5,7},{6,4},{7,5},{8,10},{9,11},{10,... | collective-permute-start | bytes 884744 | tf_op jit(solution)/shard_map/ppermute | solution.py:294
  462.0 53.7 %collective-permute-start.6 = (bf16[4,96,384]{2,1,0:T(8,128)(2,1)S(1)}, bf16[4,96,384]{2,1,0:T(8,128)(2,1)S(1)}, u32[]{:S(2)}, u32[]{:S(2)}) collective-permute-start(bf16[4,96,384]{2,1,0:T(8,128)(2,1)S(1)} %get-tuple-element.33), channel_id=1, source_target_pairs={{0,1},{1,2},{2,3},{3,0},{4,5},{5,6},{6,7},{7,4},{8,9},{9,10},{10,1... | collective-permute-start | bytes 884744 | tf_op jit(solution)/shard_map/ppermute | solution.py:294
  482.1 33.8 %collective-permute-start.2 = (bf16[4,96,384]{2,1,0:T(8,128)(2,1)S(1)}, bf16[4,96,384]{2,1,0:T(8,128)(2,1)S(1)}, u32[]{:S(2)}, u32[]{:S(2)}) collective-permute-start(bf16[4,96,384]{2,1,0:T(8,128)(2,1)S(1)} %get-tuple-element.39), channel_id=1, source_target_pairs={{0,3},{1,0},{2,1},{3,2},{4,7},{5,4},{6,5},{7,6},{8,11},{9,8},{10,9... | collective-permute-start | bytes 884744 | tf_op jit(solution)/shard_map/ppermute | solution.py:294
  482.1 62.1 %collective-permute-start.1 = (bf16[4,96,384]{2,1,0:T(8,128)(2,1)S(1)}, bf16[4,96,384]{2,1,0:T(8,128)(2,1)S(1)}, u32[]{:S(2)}, u32[]{:S(2)}) collective-permute-start(bf16[4,96,384]{2,1,0:T(8,128)(2,1)S(1)} %get-tuple-element.40), channel_id=1, source_target_pairs={{0,2},{1,3},{2,0},{3,1},{4,6},{5,7},{6,4},{7,5},{8,10},{9,11},{10,... | collective-permute-start | bytes 884744 | tf_op jit(solution)/shard_map/ppermute | solution.py:294
  495.7 48.5 %collective-permute-start = (bf16[4,96,384]{2,1,0:T(8,128)(2,1)S(1)}, bf16[4,96,384]{2,1,0:T(8,128)(2,1)S(1)}, u32[]{:S(2)}, u32[]{:S(2)}) collective-permute-start(bf16[4,96,384]{2,1,0:T(8,128)(2,1)S(1)} %get-tuple-element.41), channel_id=1, source_target_pairs={{0,1},{1,2},{2,3},{3,0},{4,5},{5,6},{6,7},{7,4},{8,9},{9,10},{10,1... | collective-permute-start | bytes 884744 | tf_op jit(solution)/shard_map/ppermute | solution.py:294
  515.7 42.3 %copy-start.7 = (bf16[4,96,384]{2,1,0:T(8,128)(2,1)}, bf16[4,96,384]{2,1,0:T(8,128)(2,1)S(1)}, u32[]{:S(2)}) copy-start(bf16[4,96,384]{2,1,0:T(8,128)(2,1)S(1)} %collective-permute-done.7.refs_3_) | copy-start | bytes 884740
  515.7 55.4 %collective-permute-start.16 = (bf16[4,96,384]{2,1,0:T(8,128)(2,1)S(1)}, bf16[4,96,384]{2,1,0:T(8,128)(2,1)S(1)}, u32[]{:S(2)}, u32[]{:S(2)}) collective-permute-start(bf16[4,96,384]{2,1,0:T(8,128)(2,1)S(1)} %copy-done.2), channel_id=1, source_target_pairs={{0,2},{1,3},{2,0},{3,1},{4,6},{5,7},{6,4},{7,5},{8,10},{9,11},{10,... | collective-permute-start | bytes 884744 | tf_op jit(solution)/shard_map/ppermute | solution.py:294
  515.7 42.3 %copy-start.8 = (bf16[4,96,384]{2,1,0:T(8,128)(2,1)}, bf16[4,96,384]{2,1,0:T(8,128)(2,1)S(1)}, u32[]{:S(2)}) copy-start(bf16[4,96,384]{2,1,0:T(8,128)(2,1)S(1)} %collective-permute-done.6.refs_2_) | copy-start | bytes 884740
  515.8 55.4 %collective-permute-start.15 = (bf16[4,96,384]{2,1,0:T(8,128)(2,1)S(1)}, bf16[4,96,384]{2,1,0:T(8,128)(2,1)S(1)}, u32[]{:S(2)}, u32[]{:S(2)}) collective-permute-start(bf16[4,96,384]{2,1,0:T(8,128)(2,1)S(1)} %copy-done.1), channel_id=1, source_target_pairs={{0,1},{1,2},{2,3},{3,0},{4,5},{5,6},{6,7},{7,4},{8,9},{9,10},{10,1... | collective-permute-start | bytes 884744 | tf_op jit(solution)/shard_map/ppermute | solution.py:294
  515.8 55.3 %collective-permute-start.14 = (bf16[4,96,384]{2,1,0:T(8,128)(2,1)S(1)}, bf16[4,96,384]{2,1,0:T(8,128)(2,1)S(1)}, u32[]{:S(2)}, u32[]{:S(2)}) collective-permute-start(bf16[4,96,384]{2,1,0:T(8,128)(2,1)S(1)} %get-tuple-element.23), channel_id=1, source_target_pairs={{0,3},{1,0},{2,1},{3,2},{4,7},{5,4},{6,5},{7,6},{8,11},{9,8},{10,9... | collective-permute-start | bytes 884744 | tf_op jit(solution)/shard_map/ppermute | solution.py:294
  544.2 27.0 %collective-permute-start.13 = (bf16[4,96,384]{2,1,0:T(8,128)(2,1)S(1)}, bf16[4,96,384]{2,1,0:T(8,128)(2,1)S(1)}, u32[]{:S(2)}, u32[]{:S(2)}) collective-permute-start(bf16[4,96,384]{2,1,0:T(8,128)(2,1)S(1)} %get-tuple-element.24), channel_id=1, source_target_pairs={{0,2},{1,3},{2,0},{3,1},{4,6},{5,7},{6,4},{7,5},{8,10},{9,11},{10,... | collective-permute-start | bytes 884744 | tf_op jit(solution)/shard_map/ppermute | solution.py:294
  544.2 27.0 %collective-permute-start.12 = (bf16[4,96,384]{2,1,0:T(8,128)(2,1)S(1)}, bf16[4,96,384]{2,1,0:T(8,128)(2,1)S(1)}, u32[]{:S(2)}, u32[]{:S(2)}) collective-permute-start(bf16[4,96,384]{2,1,0:T(8,128)(2,1)S(1)} %get-tuple-element.25), channel_id=1, source_target_pairs={{0,1},{1,2},{2,3},{3,0},{4,5},{5,6},{6,7},{7,4},{8,9},{9,10},{10,1... | collective-permute-start | bytes 884744 | tf_op jit(solution)/shard_map/ppermute | solution.py:294
  (13 other events, 120.5 us)
